TPU v7x, 32 devices: a whole 2x2x4 slice. The times are simulated.
32 devices in a mesh: dp: 16 (over z, x, core), seq: 2 (over y).
Axes of the slice: x: 2, y: 2, z: 4, core: 2. Of those that a mesh axis runs over, the one named last changes fastest.
Arguments:
- tokens: bfloat16 [16, 384, 768], P('dp', 'seq'), may hold values from -6 to 6
- segment_ids: int32 [16, 384], P('dp'), may hold values from 0 to 383, as said below
- buckets: int32 [384], replicated, may hold values from 0 to 31, as said below
- encoder: bfloat16 [16, 256, 768], P('dp', 'seq'), may hold values from -6 to 6
- norm_gains: float32 [3, 768], replicated, may hold values from 0.1 to 1.9
- rel_table: float32 [32, 12], replicated, may hold values from -4 to 4
- attn_in: bfloat16 [768, 2304], P(('dp', 'seq')), may hold values from -0.109375 to 0.109375
- attn_out: bfloat16 [768, 768], P(('dp', 'seq')), may hold values from -0.875 to 0.875
- cross_query: bfloat16 [768, 768], P(('dp', 'seq')), may hold values from -0.109375 to 0.109375
- cross_kv: bfloat16 [768, 1536], P(('dp', 'seq')), may hold values from -0.109375 to 0.109375
- cross_out: bfloat16 [768, 768], P(('dp', 'seq')), may hold values from -0.875 to 0.875
- ff_in: bfloat16 [768, 4096], P(('dp', 'seq')), may hold values from -0.21875 to 0.21875
- ff_out: bfloat16 [768, 2048], P(('dp', 'seq')), may hold values from -0.125 to 0.125
- cotangent: bfloat16 [16, 384, 768], P('dp', 'seq'), may hold values from -6 to 6
Outputs:
- block_out: bfloat16 [16, 384, 768], P('dp', 'seq')
- tokens_grad: float32 [16, 384, 768], P('dp', 'seq')
- encoder_grad: float32 [16, 256, 768], P('dp', 'seq')
- norm_gains_grad: float32 [3, 768], replicated
- rel_table_grad: float32 [32, 12], replicated
- attn_in_grad: float32 [768, 2304], P(('dp', 'seq'))
- attn_out_grad: float32 [768, 768], P(('dp', 'seq'))
- cross_query_grad: float32 [768, 768], P(('dp', 'seq'))
- cross_kv_grad: float32 [768, 1536], P(('dp', 'seq'))
- cross_out_grad: float32 [768, 768], P(('dp', 'seq'))
- ff_in_grad: float32 [768, 4096], P(('dp', 'seq'))
- ff_out_grad: float32 [768, 2048], P(('dp', 'seq'))
Inputs may be any that keep to these rules, and one draw needn't show every extreme that they name: `segment_ids`: non-decreasing along each sequence; each position holds the first position of its document; documents start only at position 0, at positions 1 to 96, or after 3 * 96, so one document covers positions 96 to 288; the last position always starts a document of its own. `buckets`: non-decreasing in the distance, 0 at distance 0 and 31 at distance 384 - 1.
All inputs are finite; a program needn't handle non-finite values.
Results may differ from a plain program's by a relative error of at most 0.024.
The roundings to bfloat16 on the way count: a program that leaves them out, or rounds other values in their place, can miss the bound.
Values may be sent and summed in bfloat16 or wider, within the bound.
A program may use at most 256 MiB of HBM per device.

v0:
```python
import jax
import jax.numpy as jnp
from jax import lax
from jax.sharding import PartitionSpec as P

H = 12
HD = 64
FF = 2048


epsilon = 1e-06
masked_value = -1000000000.0
block_limit = 512


def rms_scaled(values, gain_row):
    return (
        values * lax.rsqrt(jnp.mean(values * values, axis=-1, keepdims=True) + epsilon) * gain_row
    )


def gelu_tanh(values):
    return (
        0.5
        * values
        * (1.0 + jnp.tanh(0.7978845608028654 * (values + 0.044715 * values * values * values)))
    )


def gated(gate_act, upward):
    return gelu_tanh(gate_act) * upward


def bias_table(table_in, grid_onehot):
    return jnp.einsum("bij,bh->hij", grid_onehot, table_in, precision=lax.Precision.HIGHEST)


def score_block(queries, key_rows, rel_bias, allowed):
    scores = jnp.einsum("rhd,shd->hrs", queries, key_rows, preferred_element_type=jnp.float32)
    if rel_bias is not None:
        scores = jnp.where(allowed[None], scores + rel_bias, masked_value)
    return scores


def attend_forward(queries, key_rows, values, rel_bias, allowed):
    scores = score_block(queries, key_rows, rel_bias, allowed)
    row_top = jnp.max(scores, axis=2, keepdims=True)
    exponent = jnp.exp(scores - row_top)
    row_total = jnp.sum(exponent, axis=2, keepdims=True)
    weights_low = (exponent / row_total).astype(jnp.bfloat16)
    context = jnp.einsum("hrs,shd->rhd", weights_low, values, preferred_element_type=jnp.float32)
    return (context.astype(jnp.bfloat16), row_top + jnp.log(row_total))


def attend_backward(queries, key_rows, values, rel_bias, allowed, log_total, grad_context):
    scores = score_block(queries, key_rows, rel_bias, allowed)
    weights_full = jnp.exp(scores - log_total)
    weights_low = weights_full.astype(jnp.bfloat16)
    grad_values = jnp.einsum(
        "hrs,rhd->shd", weights_low, grad_context, preferred_element_type=jnp.float32
    )
    grad_weights = jnp.einsum(
        "rhd,shd->hrs", grad_context, values, preferred_element_type=jnp.float32
    )
    row_dot = jnp.sum(grad_weights * weights_full, axis=2, keepdims=True)
    grad_scores = (weights_full * (grad_weights - row_dot)).astype(jnp.bfloat16)
    grad_queries = jnp.einsum(
        "hrs,shd->rhd", grad_scores, key_rows, preferred_element_type=jnp.float32
    )
    grad_keys = jnp.einsum("hrs,rhd->shd", grad_scores, queries, preferred_element_type=jnp.float32)
    return (grad_queries, grad_keys, grad_values, grad_scores)


def outer_rows(left, right):
    return jnp.einsum("tc,tk->ck", left, right, preferred_element_type=jnp.float32)


def local(
    tokens,
    segment_ids,
    buckets,
    encoder,
    norm_gains,
    rel_table,
    attn_in,
    attn_out,
    cross_query,
    cross_kv,
    cross_out,
    ff_in,
    ff_out,
    cotangent,
):
    tok_count = tokens.shape[1]
    model_width = tokens.shape[2]
    length = segment_ids.shape[1]
    bucket_count = rel_table.shape[0]
    first_row = lax.axis_index("seq") * tok_count
    tok_float = tokens[0].astype(jnp.float32)
    segments = segment_ids[0]
    key_pos = jnp.arange(length, dtype=jnp.int32)
    bucket_ids = jnp.arange(bucket_count, dtype=jnp.int32)
    block_rows = min(tok_count, block_limit)

    def block_layout(block_index):
        row_start = block_index * block_rows
        query_pos = first_row + row_start + jnp.arange(block_rows, dtype=jnp.int32)
        query_seg = lax.dynamic_slice_in_dim(segments, first_row + row_start, block_rows)
        allowed = (key_pos[None, :] <= query_pos[:, None]) & (
            query_seg[:, None] == segments[None, :]
        )
        distance = jnp.maximum(query_pos[:, None] - key_pos[None, :], 0)
        bucket_grid = jnp.take(buckets, distance, axis=0)
        grid_onehot = (bucket_grid[None, :, :] == bucket_ids[:, None, None]).astype(jnp.float32)
        return (row_start, allowed, grid_onehot)

    (
        attn_in_all,
        attn_out_all,
        cross_query_all,
        cross_kv_all,
        cross_out_all,
        ff_in_all,
        ff_out_all,
    ) = (
        lax.all_gather(attn_in, ("dp", "seq"), axis=0, tiled=True),
        lax.all_gather(attn_out, ("dp", "seq"), axis=0, tiled=True),
        lax.all_gather(cross_query, ("dp", "seq"), axis=0, tiled=True),
        lax.all_gather(cross_kv, ("dp", "seq"), axis=0, tiled=True),
        lax.all_gather(cross_out, ("dp", "seq"), axis=0, tiled=True),
        lax.all_gather(ff_in, ("dp", "seq"), axis=0, tiled=True),
        lax.all_gather(ff_out, ("dp", "seq"), axis=0, tiled=True),
    )
    normed_one = rms_scaled(tok_float, norm_gains[0]).astype(jnp.bfloat16)
    qkv_local = jnp.dot(normed_one, attn_in_all, preferred_element_type=jnp.float32).astype(
        jnp.bfloat16
    )
    queries_one = qkv_local[:, :model_width].reshape(tok_count, H, HD)
    keyval_one = lax.all_gather(qkv_local[:, model_width:], "seq", axis=0, tiled=True)
    keys_one = keyval_one[:, :model_width].reshape(length, H, HD)
    values_one = keyval_one[:, model_width:].reshape(length, H, HD)
    contexts = []
    block_index = 0
    row_start, allowed, grid_onehot = block_layout(block_index)
    rel_bias = bias_table(rel_table, grid_onehot)
    context, log_total = attend_forward(queries_one, keys_one, values_one, rel_bias, allowed)
    contexts.append(context)
    totals_one = [log_total]
    context_one = contexts[0].reshape(tok_count, model_width)
    hidden_one = tok_float + jnp.dot(context_one, attn_out_all, preferred_element_type=jnp.float32)
    normed_two = rms_scaled(hidden_one, norm_gains[1]).astype(jnp.bfloat16)
    queries_flat = jnp.dot(normed_two, cross_query_all, preferred_element_type=jnp.float32).astype(
        jnp.bfloat16
    )
    queries_two = queries_flat.reshape(tok_count, H, HD)
    enc_rows = encoder[0]
    keyval_local = jnp.dot(enc_rows, cross_kv_all, preferred_element_type=jnp.float32).astype(
        jnp.bfloat16
    )
    keyval_two = lax.all_gather(keyval_local, "seq", axis=0, tiled=True)
    enc_length = keyval_two.shape[0]
    keys_two = keyval_two[:, :model_width].reshape(enc_length, H, HD)
    values_two = keyval_two[:, model_width:].reshape(enc_length, H, HD)
    contexts = []
    block_index = 0
    row_start = block_index * block_rows
    context, log_total = attend_forward(queries_two, keys_two, values_two, None, None)
    contexts.append(context)
    totals_two = [log_total]
    context_two = contexts[0].reshape(tok_count, model_width)
    hidden_two = hidden_one + jnp.dot(
        context_two, cross_out_all, preferred_element_type=jnp.float32
    )
    normed_three = rms_scaled(hidden_two, norm_gains[2]).astype(jnp.bfloat16)
    pre_act = jnp.dot(normed_three, ff_in_all, preferred_element_type=jnp.float32)
    gate_act = pre_act[:, :FF]
    upward = pre_act[:, FF:]
    mixed_act = gated(gate_act, upward).astype(jnp.bfloat16)
    layer_out = hidden_two + jnp.einsum(
        "tf,df->td", mixed_act, ff_out_all, preferred_element_type=jnp.float32
    )
    grad_out = cotangent[0].astype(jnp.float32)
    grad_branch = grad_out.astype(jnp.bfloat16)
    (
        attn_in_back,
        attn_out_back,
        cross_query_back,
        cross_kv_back,
        cross_out_back,
        ff_in_back,
        ff_out_back,
    ) = (
        attn_in_all,
        attn_out_all,
        cross_query_all,
        cross_kv_all,
        cross_out_all,
        ff_in_all,
        ff_out_all,
    )
    grad_mixed = jnp.einsum(
        "td,df->tf", grad_branch, ff_out_back, preferred_element_type=jnp.float32
    )
    gate_value, gate_pull = jax.vjp(gated, gate_act, upward)
    grad_gate, grad_up = gate_pull(grad_mixed)
    grad_pre = jnp.concatenate([grad_gate, grad_up], 1).astype(jnp.bfloat16)
    grad_normed = jnp.einsum("tk,ck->tc", grad_pre, ff_in_back, preferred_element_type=jnp.float32)
    norm_value, norm_pull = jax.vjp(rms_scaled, hidden_two, norm_gains[2])
    grad_resid, gain_three = norm_pull(grad_normed)
    grad_hidden_two = grad_out + grad_resid
    grad_branch_two = grad_hidden_two.astype(jnp.bfloat16)
    grad_context_two = jnp.einsum(
        "tk,ck->tc", grad_branch_two, cross_out_back, preferred_element_type=jnp.float32
    )
    grad_context_two = grad_context_two.astype(jnp.bfloat16).reshape(tok_count, H, HD)
    query_grads = []
    block_index = 0
    row_start = block_index * block_rows
    grad_queries, grad_keys, grad_values, grad_scores = attend_backward(
        queries_two, keys_two, values_two, None, None, totals_two[block_index], grad_context_two
    )
    query_grads.append(grad_queries)
    keys_sum = grad_keys
    values_sum = grad_values
    grad_kv_two = jnp.concatenate(
        [keys_sum.reshape(enc_length, model_width), values_sum.reshape(enc_length, model_width)], 1
    )
    grad_kv_local = lax.psum_scatter(
        grad_kv_two.astype(jnp.bfloat16), "seq", scatter_dimension=0, tiled=True
    )
    grad_queries_two = query_grads[0].reshape(tok_count, model_width).astype(jnp.bfloat16)
    encoder_grad = jnp.einsum(
        "tk,ck->tc", grad_kv_local, cross_kv_back, preferred_element_type=jnp.float32
    )
    grad_normed = jnp.einsum(
        "tk,ck->tc", grad_queries_two, cross_query_back, preferred_element_type=jnp.float32
    )
    norm_value, norm_pull = jax.vjp(rms_scaled, hidden_one, norm_gains[1])
    grad_resid, gain_two = norm_pull(grad_normed)
    grad_hidden_one = grad_hidden_two + grad_resid
    grad_branch_one = grad_hidden_one.astype(jnp.bfloat16)
    grad_context_one = jnp.einsum(
        "tk,ck->tc", grad_branch_one, attn_out_back, preferred_element_type=jnp.float32
    )
    grad_context_one = grad_context_one.astype(jnp.bfloat16).reshape(tok_count, H, HD)
    query_grads = []
    block_index = 0
    row_start, allowed, grid_onehot = block_layout(block_index)
    rel_bias = bias_table(rel_table, grid_onehot)
    grad_queries, grad_keys, grad_values, grad_scores = attend_backward(
        queries_one,
        keys_one,
        values_one,
        rel_bias,
        allowed,
        totals_one[block_index],
        grad_context_one,
    )
    table_grad = jnp.einsum(
        "hij,bij->bh", grad_scores.astype(jnp.float32), grid_onehot, precision=lax.Precision.HIGHEST
    )
    query_grads.append(grad_queries)
    grad_kv_one = jnp.concatenate(
        [grad_keys.reshape(length, model_width), grad_values.reshape(length, model_width)], 1
    )
    grad_kv_own = lax.psum_scatter(
        grad_kv_one.astype(jnp.bfloat16), "seq", scatter_dimension=0, tiled=True
    )
    grad_queries_one = query_grads[0].reshape(tok_count, model_width).astype(jnp.bfloat16)
    grad_qkv = jnp.concatenate([grad_queries_one, grad_kv_own], 1)
    grad_normed = jnp.einsum(
        "tk,ck->tc", grad_qkv, attn_in_back, preferred_element_type=jnp.float32
    )
    norm_value, norm_pull = jax.vjp(rms_scaled, tok_float, norm_gains[0])
    grad_resid, gain_one = norm_pull(grad_normed)
    tokens_grad = grad_hidden_one + grad_resid
    all_grads = lax.psum_scatter(
        jnp.concatenate(
            [
                jnp.concatenate(
                    [outer_rows(normed_one, grad_qkv), outer_rows(context_one, grad_branch_one)], 1
                ),
                jnp.concatenate(
                    [
                        outer_rows(normed_two, grad_queries_two),
                        outer_rows(enc_rows, grad_kv_local),
                        outer_rows(context_two, grad_branch_two),
                    ],
                    1,
                ),
                jnp.concatenate(
                    [outer_rows(normed_three, grad_pre), outer_rows(grad_branch, mixed_act)], 1
                ),
            ],
            1,
        ),
        ("dp", "seq"),
        scatter_dimension=0,
        tiled=True,
    )
    gains_sum, table_sum = lax.psum(
        (jnp.stack([gain_one, gain_two, gain_three], 0), table_grad), ("dp", "seq")
    )
    return (
        layer_out.astype(jnp.bfloat16)[None],
        tokens_grad[None],
        encoder_grad[None],
        gains_sum,
        table_sum,
        all_grads[:, : 3 * model_width],
        all_grads[:, 3 * model_width : 4 * model_width],
        all_grads[:, 4 * model_width : 5 * model_width],
        all_grads[:, 5 * model_width : 7 * model_width],
        all_grads[:, 7 * model_width : 8 * model_width],
        all_grads[:, 8 * model_width : 8 * model_width + 2 * FF],
        all_grads[:, 8 * model_width + 2 * FF :],
    )


def solution(mesh):
    return jax.shard_map(
        local,
        mesh=mesh,
        in_specs=(
            P("dp", "seq", None),
            P("dp", None),
            P(),
            P("dp", "seq", None),
            P(),
            P(),
            P(("dp", "seq"), None),
            P(("dp", "seq"), None),
            P(("dp", "seq"), None),
            P(("dp", "seq"), None),
            P(("dp", "seq"), None),
            P(("dp", "seq"), None),
            P(("dp", "seq"), None),
            P("dp", "seq", None),
        ),
        out_specs=(
            P("dp", "seq", None),
            P("dp", "seq", None),
            P("dp", "seq", None),
            P(),
            P(),
            P(("dp", "seq"), None),
            P(("dp", "seq"), None),
            P(("dp", "seq"), None),
            P(("dp", "seq"), None),
            P(("dp", "seq"), None),
            P(("dp", "seq"), None),
            P(("dp", "seq"), None),
        ),
        check_vma=False,
    )
```

profile of v0, /device:TPU:0, one launch (start us, length us, event | category | flops | bytes accessed | tf_op | source)
XLA Modules:
  0.0 1058.0 jit_solution(5664509729326514100)
XLA Ops:
  10.7 63.2 %all-gather.9.cloned.1.call-done = bf16[768,2304]{1,0:T(8,128)(2,1)} async-done(((bf16[24,2304]{1,0:T(8,128)(2,1)}), bf16[768,2304]{1,0:T(8,128)(2,1)}) %all-gather.9.cloned.1.call-update) | async-done | bytes 3538960 | tf_op jit(solution)/shard_map/all_gather | solution.py:126
  73.9 3.0 convolution_convert_fusion
  81.6 459.2 %gather_fusion = s32[73728]{0:T(1024)S(1)} fusion(s32[384]{0:T(512)S(1)} %copy-done.1, s32[73728]{0:T(1024)S(1)} %broadcast_clamp_fusion), kind=kCustom, calls=%fused_computation.clone | custom fusion | bytes 884736 | tf_op jit(solution)/shard_map/jit(_take)/gather | solution.py:113
  541.7 4.5 fusion.1
  546.2 2.1 convolution_convert_fusion.1
  548.3 12.0 %all_gather.31 = bf16[256,1536]{1,0:T(8,128)(2,1)S(1)} all-gather(bf16[128,1536]{1,0:T(8,128)(2,1)S(1)} %convolution_convert_fusion.1), channel_id=1, replica_groups=mesh['dp'=16,'seq'=2] {'seq'}, dimensions={0}, use_global_device_ids=true | all-gather | bytes 1179648 | tf_op jit(solution)/shard_map/all_gather | solution.py:160
  562.5 1.4 fusion.65
  564.6 4.4 fusion.67
  570.8 1.6 fusion.23
  572.4 1.9 multiply_reduce_fusion.7
  574.4 1.7 convolution_convert_fusion.10
  577.0 1.9 fusion.68
  579.8 1.8 convolution_convert_fusion.7
  581.6 2.6 multiply_reduce_fusion.6
  584.3 6.2 fusion.63
  590.5 6.1 fusion.17
  596.6 2.4 multiply_reduce_fusion.2
  600.4 1.3 convolution_convert_fusion.9
  601.7 1.9 copy.71
  603.6 2.3 multiply_reduce_fusion.1
  605.9 1.3 convolution_convert_fusion.3
  607.2 13.7 %multiply_convert_fusion.1 = bf16[12,192,256]{2,1,0:T(8,128)(2,1)S(1)} fusion(f32[12,192,256]{2,1,0:T(8,128)S(1)} %get-tuple-element.44, f32[12,192,256]{2,1,0:T(8,128)S(1)} %get-tuple-element.39, f32[12,192]{1,0:T(8,128)S(1)} %get-tuple-element.43, f32[12,192]{1,0:T(8,128)S(1)} %log_add_fusion.1), kind=kLoop, calls=%fused_computation.24 | loop fusion | flops 2359296 | bytes 5916672 | tf_op jit(solution)/shard_map/convert_element_type | solution.py:66
  627.4 3.4 multiply_reduce_fusion
  634.3 2.5 copy.83
  636.9 1.6 convolution_convert_fusion.5
  638.5 5.2 reduce-scatter.12.cloned.1.call-done
  643.7 3.9 convolution_bitcast_fusion
  647.6 6.1 copy.77
  653.7 13.9 %reduce-scatter.10.cloned.1.call-done = bf16[192,1536]{1,0:T(8,128)(2,1)} async-done(((bf16[384,1536]{1,0:T(8,128)(2,1)}), bf16[192,1536]{1,0:T(8,128)(2,1)}) %reduce-scatter.10.cloned.1.call-update) | async-done | bytes 589840
  667.7 2.3 copy.84
  670.0 5.5 convolution_dynamic-update-slice_fusion.1
  675.5 1.9 convolution_dynamic-update-slice_fusion.4
  677.4 2.0 convolution_dynamic-update-slice_fusion.3
  679.4 2.5 constant_dynamic-update-slice_fusion
  681.9 1.9 convolution_dynamic-update-slice_fusion.2
  683.9 6.5 convolution_dynamic-update-slice_fusion
  690.4 3.7 bitcast_dynamic-update-slice_fusion
  694.2 3.2 fusion.28
  697.4 1.9 fusion.27
  699.4 1.6 convolution_bitcast_fusion.1
  701.5 1.5 fusion.36
  703.1 39.6 %all-reduce = (f32[3,768]{1,0:T(4,128)}, f32[32,12]{0,1:T(8,128)}) all-reduce(f32[3,768]{1,0:T(4,128)S(1)} %pad_maximum_fusion.8, f32[32,12]{0,1:T(8,128)S(1)} %fusion.28), channel_id=1, replica_groups=mesh['dp'=16,'seq'=2] {'dp','seq'}, use_global_device_ids=true, to_apply=%region_17.19 | all-reduce | flops 2688 | bytes 21504 | tf_op jit(solution)/shard_map/psum | solution.py:301
  743.7 299.4 %reduce-scatter.8.cloned.1.call-done = f32[24,12288]{1,0:T(8,128)} async-done(((f32[768,12288]{1,0:T(8,128)}), f32[24,12288]{1,0:T(8,128)}) %reduce-scatter.8.cloned.1.call-update) | async-done | bytes 1179664 | tf_op jit(solution)/shard_map/reduce_scatter | solution.py:277
  1043.0 1.6 slice.85
  1044.7 1.6 fusion.64
  1046.3 1.6 slice.88
  1047.9 1.8 slice.90
  1049.7 1.6 slice.91
  (186 shorter events, 28.4 us)
Async XLA Ops:
  7.2 539.0 %copy-start = (bf16[1,128,768]{2,1,0:T(8,128)(2,1)S(1)}, bf16[1,128,768]{2,1,0:T(8,128)(2,1)}, u32[]{:S(2)}) copy-start(bf16[1,128,768]{2,1,0:T(8,128)(2,1)} %param.19) | copy-start | bytes 589828
  7.2 66.7 %all-gather.9.cloned.1.call-start = ((), (), s32[]{:S(2)}) async-start(), calls=%async_computation.3 | async-start | bytes 3649536 | tf_op jit(solution)/shard_map/all_gather | solution.py:126
  7.9 538.3 %all-gather.15.cloned.1.call-start = ((), (), s32[]{:S(2)}) async-start(), calls=%async_computation.6 | async-start | bytes 2433024 | tf_op jit(solution)/shard_map/all_gather | solution.py:129
  8.7 553.8 %all-gather.11.cloned.1.call-start = ((), (), s32[]{:S(2)}) async-start(), calls=%async_computation.4 | async-start | bytes 1769472 | tf_op jit(solution)/shard_map/all_gather | solution.py:139
  10.7 66.2 %copy-start.48 = (f32[192]{0:T(256)}, f32[192]{0:T(256)S(1)}, u32[]{:S(2)}) copy-start(f32[192]{0:T(256)S(1)} %fusion.41) | copy-start | bytes 2308
  76.9 4.4 copy-start.51
  76.9 4.6 copy-start.1
  77.8 494.6 %all-gather.13.cloned.1.call-start = ((), (), s32[]{:S(2)}) async-start(), calls=%async_computation.5 | async-start | bytes 1216512 | tf_op jit(solution)/shard_map/all_gather | solution.py:127
  78.4 496.0 %all-gather.17.cloned.1.call-start = ((), (), s32[]{:S(2)}) async-start(), calls=%async_computation.7 | async-start | bytes 1216512 | tf_op jit(solution)/shard_map/all_gather | solution.py:128
  79.0 502.6 %all-gather.19.cloned.1.call-start = ((), (), s32[]{:S(2)}) async-start(), calls=%async_computation.8 | async-start | bytes 1216512 | tf_op jit(solution)/shard_map/all_gather | solution.py:130
  79.6 504.7 %all-gather.21.cloned.1.call-start = ((), (), s32[]{:S(2)}) async-start(), calls=%async_computation.9 | async-start | bytes 6488064 | tf_op jit(solution)/shard_map/all_gather | solution.py:131
  80.3 510.1 %all-gather.23.cloned.1.call-start = ((), (), s32[]{:S(2)}) async-start(), calls=%async_computation.10 | async-start | bytes 3244032 | tf_op jit(solution)/shard_map/all_gather | solution.py:132
  81.1 562.7 %reduce-scatter.12.cloned.1.call-start = ((), (), s32[]{:S(2)}) async-start(), calls=%async_computation.13 | async-start | bytes 1179648
  81.6 460.2 %copy-start.50 = (f32[32,12]{0,1:T(8,128)S(1)}, f32[32,12]{0,1:T(8,128)}, u32[]{:S(2)}) copy-start(f32[32,12]{0,1:T(8,128)} %param.21) | copy-start | bytes 4612
  562.5 2.1 copy-start.22
  564.2 6.0 copy-start.32
  564.6 4.4 copy-start.15
  572.4 4.6 copy-start.37
  577.0 2.8 copy-start.40
  590.4 6.1 copy-start.4
  590.5 6.1 copy-start.6
  596.5 2.4 copy-start.44
  596.5 2.4 copy-start.46
  596.6 2.4 copy-start.41
  603.6 2.3 copy-start.29
  607.2 13.7 %copy-start.27 = (bf16[256,768]{0,1:T(8,128)(2,1)S(1)}, bf16[256,768]{0,1:T(8,128)(2,1)}, u32[]{:S(2)}) copy-start(bf16[256,768]{0,1:T(8,128)(2,1)} %copy.70) | copy-start | bytes 1179652
  607.2 14.2 %copy-start.28 = (bf16[192,768]{0,1:T(8,128)(2,1)S(1)}, bf16[192,768]{0,1:T(8,128)(2,1)}, u32[]{:S(2)}) copy-start(bf16[192,768]{0,1:T(8,128)(2,1)} %copy.69) | copy-start | bytes 884740
  624.9 2.5 copy-start.33
  627.3 40.3 %reduce-scatter.10.cloned.1.call-start = ((), (), s32[]{:S(2)}) async-start(), calls=%async_computation.12 | async-start | bytes 1769472
  627.4 3.4 copy-start.3
  634.3 2.6 copy-start.16
  636.8 406.2 %reduce-scatter.8.cloned.1.call-start = ((), (), s32[]{:S(2)}) async-start(), calls=%async_computation.11 | async-start | bytes 38928384 | tf_op jit(solution)/shard_map/reduce_scatter | solution.py:277
  667.7 11.8 %slice-start = ((s8[4718592]{0:T(1024)(128)(4,1)}), s8[524288]{0:T(1024)(128)(4,1)S(1)}, s32[]{:S(2)}) async-start(s8[4718592]{0:T(1024)(128)(4,1)} %bitcast.121), calls=%async_computation.14 | async-start | bytes 1048576
  670.0 5.5 copy-start.9
  670.0 5.5 copy-start.38
  670.0 9.5 slice-start.1
  679.4 2.5 copy-start.13
  679.4 2.5 copy-start.35
  681.9 1.9 copy-start.45
  683.9 6.6 copy-start.17
  683.9 6.6 copy-start.42
  694.2 3.2 copy-start.18
  694.2 3.2 copy-start.30
  694.2 5.2 copy-start.39
  697.4 3.6 copy-start.24
  699.4 2.2 copy-start.34
  701.5 41.1 %copy-start.49 = (f32[192]{0:T(256)S(1)}, f32[192]{0:T(256)}, u32[]{:S(2)}) copy-start(f32[192]{0:T(256)} %copy-done.48) | copy-start | bytes 2308
  701.5 41.1 %copy-start.10 = (f32[192,768]{1,0:T(8,128)S(1)}, f32[192,768]{1,0:T(8,128)}, u32[]{:S(2)}) copy-start(f32[192,768]{1,0:T(8,128)} %copy-done.8) | copy-start | bytes 1769476
  (17 other events, 26.8 us)
Sparse Core Ops, SparseCore 0:
  10.9 62.8 all-gather.8
  76.8 56.1 all-gather.14
  135.1 21.6 all-gather.10
  159.6 54.1 all-gather.12
  216.5 53.0 all-gather.16
  272.4 53.0 all-gather.18
  328.4 68.4 all-gather.20
  399.8 57.6 all-gather.22
  627.5 16.2 reduce-scatter.11
  645.9 21.7 reduce-scatter.9
  694.3 348.7 reduce-scatter.7
where the time goes:
time: 1060 us
  local copies, waits for them, and re-layouts  495 us (47%)
  waiting for transfers between devices  386 us (36%)
  matrix products  88 us (8%)
  blocking collectives  51.5 us (5%)
  other arithmetic  21.8 us (2%)
  between operations  14.9 us (1%)
    gather x2, local copies, waits for them, and re-layouts, block_layout(): bucket_grid = jnp.take(buckets, distance, axis=0)  459 us
    reduce_scatter x1, waiting for transfers between devices, local(): lax.psum_scatter(jnp.concatenate([jnp.concatenate([outer_rows(normed_one,...  299 us
    all_gather x1, waiting for transfers between devices, local(): lax.all_gather(attn_in, ('dp', 'seq'), axis=0, tiled=True)  63.2 us
    psum x1, blocking collectives, local(): lax.psum((jnp.stack([gain_one, gain_two, gain_three], 0), table_grad), ('...  39.6 us
    dot_general x7, matrix products, outer_rows(): jnp.einsum('tc,tk->ck', left, right, preferred_element_type=jnp.float32)  25.5 us
    unnamed x13, waiting for transfers between devices  23.5 us
  transfers between devices with their start and end apart: 11, of which 4 were waited for; matrix products, arithmetic and copies ran while one was open for 50% of the time, Pallas kernels for 0%

commit v1 on v0

v1 whole, which is shorter than its diff:
```python
import functools

import jax
import jax.numpy as jnp
from jax import lax
from jax.sharding import PartitionSpec as P

H = 12
HD = 64
FF = 2048


epsilon = 1e-06
masked_value = -1000000000.0


def rms_scaled(values, gain_row):
    return (
        values * lax.rsqrt(jnp.mean(values * values, axis=-1, keepdims=True) + epsilon) * gain_row
    )


def gelu_tanh(values):
    return (
        0.5
        * values
        * (1.0 + jnp.tanh(0.7978845608028654 * (values + 0.044715 * values * values * values)))
    )


def gated(gate_act, upward):
    return gelu_tanh(gate_act) * upward


def bias_table(table_in, grid_onehot):
    return jnp.einsum("bij,bh->hij", grid_onehot, table_in, precision=lax.Precision.HIGHEST)


def attend_forward(queries, key_rows, values, rel_bias, allowed):
    scores = jnp.einsum("rhd,shd->hrs", queries, key_rows, preferred_element_type=jnp.float32)
    if rel_bias is not None:
        scores = jnp.where(allowed[None], scores + rel_bias, masked_value)
    row_top = jnp.max(scores, axis=2, keepdims=True)
    exponent = jnp.exp(scores - row_top)
    row_total = jnp.sum(exponent, axis=2, keepdims=True)
    weights_full = exponent / row_total
    context = jnp.einsum(
        "hrs,shd->rhd",
        weights_full.astype(jnp.bfloat16),
        values,
        preferred_element_type=jnp.float32,
    )
    return (context.astype(jnp.bfloat16), weights_full)


def attend_backward(queries, key_rows, values, weights_full, grad_context):
    weights_low = weights_full.astype(jnp.bfloat16)
    grad_values = jnp.einsum(
        "hrs,rhd->shd", weights_low, grad_context, preferred_element_type=jnp.float32
    )
    grad_weights = jnp.einsum(
        "rhd,shd->hrs", grad_context, values, preferred_element_type=jnp.float32
    )
    row_dot = jnp.sum(grad_weights * weights_full, axis=2, keepdims=True)
    grad_scores = (weights_full * (grad_weights - row_dot)).astype(jnp.bfloat16)
    grad_queries = jnp.einsum(
        "hrs,shd->rhd", grad_scores, key_rows, preferred_element_type=jnp.float32
    )
    grad_keys = jnp.einsum("hrs,rhd->shd", grad_scores, queries, preferred_element_type=jnp.float32)
    return (grad_queries, grad_keys, grad_values, grad_scores)


def outer_rows(left, right):
    return jnp.einsum("tc,tk->ck", left, right, preferred_element_type=jnp.float32).astype(
        jnp.bfloat16
    )


axes = ("dp", "seq")


def swap_bit(values, bit, devices):
    return lax.ppermute(values, axes, [(at, at ^ (1 << bit)) for at in range(devices)])


def bit_order(bits, turn):
    rest = [0] + list(range(2, bits))
    turn = turn % len(rest)
    return [1] + rest[turn:] + rest[:turn]


def scatter_sum(values, order, devices, index):
    bits = len(order)
    values = values.reshape((2,) * bits + (values.shape[0] // devices, values.shape[1]))
    left = list(range(bits - 1, -1, -1))
    for bit in order:
        place = left.index(bit)
        mine = (index >> bit) & 1
        kept = lax.dynamic_index_in_dim(values, mine, place, keepdims=False)
        sent = lax.dynamic_index_in_dim(values, 1 - mine, place, keepdims=False)
        total = kept.astype(jnp.float32) + swap_bit(sent, bit, devices).astype(jnp.float32)
        left.remove(bit)
        values = total.astype(jnp.bfloat16) if left else total
    return values


def full_sum(values, bits, devices):
    for bit in range(bits):
        values = values + swap_bit(values, bit, devices)
    return values


def local(
    devices,
    tokens,
    segment_ids,
    buckets,
    encoder,
    norm_gains,
    rel_table,
    attn_in,
    attn_out,
    cross_query,
    cross_kv,
    cross_out,
    ff_in,
    ff_out,
    cotangent,
):
    bits = devices.bit_length() - 1
    tok_count = tokens.shape[1]
    model_width = tokens.shape[2]
    enc_count = encoder.shape[1]
    my_seq = lax.axis_index("seq")
    index = lax.axis_index("dp") * 2 + my_seq

    def scattered(values, turn):
        return scatter_sum(values, bit_order(bits, turn), devices, index)

    shards = (attn_in, attn_out, cross_query, cross_kv, cross_out, ff_in, ff_out)
    gathered = lax.all_gather(jnp.concatenate(shards, 1), axes, axis=0, tiled=True)
    whole = []
    column = 0
    for shard in shards:
        whole.append(gathered[:, column : column + shard.shape[1]])
        column += shard.shape[1]
    (
        attn_in_all,
        attn_out_all,
        cross_query_all,
        cross_kv_all,
        cross_out_all,
        ff_in_all,
        ff_out_all,
    ) = whole

    tokens_both = jnp.concatenate([tokens[0], swap_bit(tokens[0], 0, devices)], 0)
    enc_both = jnp.concatenate([encoder[0], swap_bit(encoder[0], 0, devices)], 0)
    tok_float = tokens[0].astype(jnp.float32)
    segments = segment_ids[0]
    own_start = my_seq * tok_count
    other_start = (1 - my_seq) * tok_count
    steps = jnp.arange(tok_count, dtype=jnp.int32)
    query_pos = own_start + steps
    key_pos = jnp.concatenate([query_pos, other_start + steps])
    query_seg = lax.dynamic_slice_in_dim(segments, own_start, tok_count)
    key_seg = jnp.concatenate(
        [query_seg, lax.dynamic_slice_in_dim(segments, other_start, tok_count)]
    )
    allowed = (key_pos[None, :] <= query_pos[:, None]) & (query_seg[:, None] == key_seg[None, :])
    distance = jnp.maximum(query_pos[:, None] - key_pos[None, :], 0)
    bucket_ids = jnp.arange(rel_table.shape[0], dtype=jnp.int32)
    range_from = jnp.sum((buckets[None, :] < bucket_ids[:, None]).astype(jnp.int32), axis=1)
    range_to = jnp.sum((buckets[None, :] <= bucket_ids[:, None]).astype(jnp.int32), axis=1)
    grid_onehot = (
        (distance[None] >= range_from[:, None, None]) & (distance[None] < range_to[:, None, None])
    ).astype(jnp.float32)
    rel_bias = bias_table(rel_table, grid_onehot)

    normed_both = rms_scaled(tokens_both.astype(jnp.float32), norm_gains[0]).astype(jnp.bfloat16)
    qkv_both = jnp.dot(normed_both, attn_in_all, preferred_element_type=jnp.float32).astype(
        jnp.bfloat16
    )
    queries_one = qkv_both[:tok_count, :model_width].reshape(tok_count, H, HD)
    keys_one = qkv_both[:, model_width : 2 * model_width].reshape(2 * tok_count, H, HD)
    values_one = qkv_both[:, 2 * model_width :].reshape(2 * tok_count, H, HD)
    context, weights_one = attend_forward(queries_one, keys_one, values_one, rel_bias, allowed)
    context_one = context.reshape(tok_count, model_width)
    hidden_one = tok_float + jnp.dot(context_one, attn_out_all, preferred_element_type=jnp.float32)
    normed_two = rms_scaled(hidden_one, norm_gains[1]).astype(jnp.bfloat16)
    queries_two = (
        jnp.dot(normed_two, cross_query_all, preferred_element_type=jnp.float32)
        .astype(jnp.bfloat16)
        .reshape(tok_count, H, HD)
    )
    keyval_two = jnp.dot(enc_both, cross_kv_all, preferred_element_type=jnp.float32).astype(
        jnp.bfloat16
    )
    keys_two = keyval_two[:, :model_width].reshape(2 * enc_count, H, HD)
    values_two = keyval_two[:, model_width:].reshape(2 * enc_count, H, HD)
    context, weights_two = attend_forward(queries_two, keys_two, values_two, None, None)
    context_two = context.reshape(tok_count, model_width)
    hidden_two = hidden_one + jnp.dot(
        context_two, cross_out_all, preferred_element_type=jnp.float32
    )
    normed_three = rms_scaled(hidden_two, norm_gains[2]).astype(jnp.bfloat16)
    pre_act = jnp.dot(normed_three, ff_in_all, preferred_element_type=jnp.float32)
    gate_act = pre_act[:, :FF]
    upward = pre_act[:, FF:]
    mixed_act = gated(gate_act, upward).astype(jnp.bfloat16)
    layer_out = hidden_two + jnp.einsum(
        "tf,df->td", mixed_act, ff_out_all, preferred_element_type=jnp.float32
    )
    grad_out = cotangent[0].astype(jnp.float32)
    grad_branch = cotangent[0]
    ff_out_grad = scattered(outer_rows(grad_branch, mixed_act), 0)
    grad_mixed = jnp.einsum(
        "td,df->tf", grad_branch, ff_out_all, preferred_element_type=jnp.float32
    )
    gate_value, gate_pull = jax.vjp(gated, gate_act, upward)
    grad_gate, grad_up = gate_pull(grad_mixed)
    grad_gate = grad_gate.astype(jnp.bfloat16)
    grad_up = grad_up.astype(jnp.bfloat16)
    gate_grad = scattered(outer_rows(normed_three, grad_gate), 1)
    up_grad = scattered(outer_rows(normed_three, grad_up), 2)
    grad_pre = jnp.concatenate([grad_gate, grad_up], 1)
    grad_normed = jnp.einsum("tk,ck->tc", grad_pre, ff_in_all, preferred_element_type=jnp.float32)
    norm_value, norm_pull = jax.vjp(rms_scaled, hidden_two, norm_gains[2])
    grad_resid, gain_three = norm_pull(grad_normed)
    grad_hidden_two = grad_out + grad_resid
    grad_branch_two = grad_hidden_two.astype(jnp.bfloat16)
    grad_context_two = jnp.einsum(
        "tk,ck->tc", grad_branch_two, cross_out_all, preferred_element_type=jnp.float32
    )
    grad_context_two = grad_context_two.astype(jnp.bfloat16).reshape(tok_count, H, HD)
    grad_queries, grad_keys, grad_values, grad_scores = attend_backward(
        queries_two, keys_two, values_two, weights_two, grad_context_two
    )
    grad_kv_two = jnp.concatenate(
        [
            grad_keys.reshape(2 * enc_count, model_width),
            grad_values.reshape(2 * enc_count, model_width),
        ],
        1,
    )
    kv_two_low = grad_kv_two.astype(jnp.bfloat16)
    cross_grads = scattered(
        jnp.concatenate(
            [outer_rows(enc_both, kv_two_low), outer_rows(context_two, grad_branch_two)], 1
        ),
        1,
    )
    grad_kv_local = (
        grad_kv_two[:enc_count]
        + swap_bit(kv_two_low[enc_count:], 0, devices).astype(jnp.float32)
    ).astype(jnp.bfloat16)
    grad_queries_two = grad_queries.reshape(tok_count, model_width).astype(jnp.bfloat16)
    encoder_grad = jnp.einsum(
        "tk,ck->tc", grad_kv_local, cross_kv_all, preferred_element_type=jnp.float32
    )
    grad_normed = jnp.einsum(
        "tk,ck->tc", grad_queries_two, cross_query_all, preferred_element_type=jnp.float32
    )
    norm_value, norm_pull = jax.vjp(rms_scaled, hidden_one, norm_gains[1])
    grad_resid, gain_two = norm_pull(grad_normed)
    grad_hidden_one = grad_hidden_two + grad_resid
    grad_branch_one = grad_hidden_one.astype(jnp.bfloat16)
    middle_grads = scattered(
        jnp.concatenate(
            [outer_rows(normed_two, grad_queries_two), outer_rows(context_one, grad_branch_one)], 1
        ),
        2,
    )
    grad_context_one = jnp.einsum(
        "tk,ck->tc", grad_branch_one, attn_out_all, preferred_element_type=jnp.float32
    )
    grad_context_one = grad_context_one.astype(jnp.bfloat16).reshape(tok_count, H, HD)
    grad_queries, grad_keys, grad_values, grad_scores = attend_backward(
        queries_one, keys_one, values_one, weights_one, grad_context_one
    )
    grad_keys = grad_keys.reshape(2 * tok_count, model_width)
    grad_values = grad_values.reshape(2 * tok_count, model_width)
    keys_low = grad_keys.astype(jnp.bfloat16)
    values_low = grad_values.astype(jnp.bfloat16)
    grad_queries_one = grad_queries.reshape(tok_count, model_width).astype(jnp.bfloat16)
    in_grads = [
        scattered(outer_rows(normed_both, values_low), 0),
        scattered(outer_rows(normed_both, keys_low), 1),
        scattered(outer_rows(normed_both[:tok_count], grad_queries_one), 2),
    ]
    other_part = swap_bit(
        jnp.concatenate([keys_low[tok_count:], values_low[tok_count:]], 1), 0, devices
    ).astype(jnp.float32)
    grad_kv_own = (
        jnp.concatenate([grad_keys[:tok_count], grad_values[:tok_count]], 1) + other_part
    ).astype(jnp.bfloat16)
    table_grad = jnp.einsum(
        "hij,bij->bh", grad_scores.astype(jnp.float32), grid_onehot, precision=lax.Precision.HIGHEST
    )
    grad_qkv = jnp.concatenate([grad_queries_one, grad_kv_own], 1)
    grad_normed = jnp.einsum("tk,ck->tc", grad_qkv, attn_in_all, preferred_element_type=jnp.float32)
    norm_value, norm_pull = jax.vjp(rms_scaled, tok_float, norm_gains[0])
    grad_resid, gain_one = norm_pull(grad_normed)
    tokens_grad = grad_hidden_one + grad_resid
    small = jnp.concatenate([gain_one, gain_two, gain_three, table_grad.reshape(-1)])
    small = full_sum(small, bits, devices)
    return (
        layer_out.astype(jnp.bfloat16)[None],
        tokens_grad[None],
        encoder_grad[None],
        small[: 3 * model_width].reshape(3, model_width),
        small[3 * model_width :].reshape(rel_table.shape),
        jnp.concatenate([in_grads[2], in_grads[1], in_grads[0]], 1),
        middle_grads[:, model_width:],
        middle_grads[:, :model_width],
        cross_grads[:, : 2 * model_width],
        cross_grads[:, 2 * model_width :],
        jnp.concatenate([gate_grad, up_grad], 1),
        ff_out_grad,
    )


def solution(mesh):
    return jax.shard_map(
        functools.partial(local, mesh.devices.size),
        mesh=mesh,
        in_specs=(
            P("dp", "seq", None),
            P("dp", None),
            P(),
            P("dp", "seq", None),
            P(),
            P(),
            P(("dp", "seq"), None),
            P(("dp", "seq"), None),
            P(("dp", "seq"), None),
            P(("dp", "seq"), None),
            P(("dp", "seq"), None),
            P(("dp", "seq"), None),
            P(("dp", "seq"), None),
            P("dp", "seq", None),
        ),
        out_specs=(
            P("dp", "seq", None),
            P("dp", "seq", None),
            P("dp", "seq", None),
            P(),
            P(),
            P(("dp", "seq"), None),
            P(("dp", "seq"), None),
            P(("dp", "seq"), None),
            P(("dp", "seq"), None),
            P(("dp", "seq"), None),
            P(("dp", "seq"), None),
            P(("dp", "seq"), None),
        ),
        check_vma=False,
    )
```

time: 1060 us -> 522 us (0.49)
  local copies, waits for them, and re-layouts: 495 us -> 71.7 us
  waiting for transfers between devices: 386 us -> 232 us
  starting transfers between devices: 0.43 us -> 53.3 us
  blocking collectives: 51.5 us -> 0 us
  matrix products: 88 us -> 109 us
  other arithmetic: 21.8 us -> 33.2 us
    gather x2 -> x0, local copies, waits for them, and re-layouts: 459 us -> none  [block_layout(): bucket_grid = jnp.take(buckets, distance, axis=0)]
    reduce_scatter x1 -> x0, waiting for transfers between devices: 299 us -> none  [local(): lax.psum_scatter(jnp.concatenate([jnp.concatenate([outer_rows(normed_one,...]
    ppermute x0 -> x49, waiting for transfers between devices: none -> 116 us  [swap_bit(): lax.ppermute(values, axes, [(at, at ^ 1 << bit) for at in range(devices)])]
    ppermute x0 -> x49, starting transfers between devices: none -> 53.2 us  [swap_bit(): lax.ppermute(values, axes, [(at, at ^ 1 << bit) for at in range(devices)])]
    all_gather x8 -> x1, waiting for transfers between devices: 63.2 us -> 116 us  [local(): lax.all_gather(jnp.concatenate(shards, 1), axes, axis=0, tiled=True)]
    psum x1 -> x0, blocking collectives: 39.6 us -> none  [local(): lax.psum((jnp.stack([gain_one, gain_two, gain_three], 0), table_grad), ('...]
    unnamed x13 -> x1, waiting for transfers between devices: 23.5 us -> 0.02 us
    dynamic_slice x1 -> x15, local copies, waits for them, and re-layouts: 0.08 us -> 20.1 us  [the longest x7 10.8 us: scatter_sum(): kept = lax.dynamic_index_in_dim(values, mine, place, keepdims=False)]
  transfers between devices with their start and end apart: 11 -> 50, of which waited for: 4 -> 28; matrix products, arithmetic and copies ran while one was open for 50% -> 18% of each run, Pallas kernels for 0% -> 0%
where the time goes in v1:
time: 522 us; the launch traced here: 515 us
  waiting for transfers between devices  232 us (44%)
  matrix products  109 us (21%)
  local copies, waits for them, and re-layouts  71.7 us (14%)
  starting transfers between devices  53.3 us (10%)
  other arithmetic  33.2 us (6%)
  between operations  15.7 us (3%)
    all_gather x1, waiting for transfers between devices, local(): lax.all_gather(jnp.concatenate(shards, 1), axes, axis=0, tiled=True)  116 us
    ppermute x49, waiting for transfers between devices, swap_bit(): lax.ppermute(values, axes, [(at, at ^ 1 << bit) for at in range(devices)])  116 us
    ppermute x49, starting transfers between devices, swap_bit(): lax.ppermute(values, axes, [(at, at ^ 1 << bit) for at in range(devices)])  53.2 us
    unnamed x189, local copies, waits for them, and re-layouts  15.6 us
    convert_element_type x32, other arithmetic, scatter_sum(): values = total.astype(jnp.bfloat16) if left else total  14.8 us
    dot_general x10, matrix products, outer_rows(): jnp.einsum('tc,tk->ck', left, right, preferred_element_type=jnp.float32)  13.4 us
    dot_general x2, matrix products, attend_forward(): jnp.einsum('hrs,shd->rhd', weights_full.astype(jnp.bfloat16), values, pre...  11.4 us
    dynamic_slice x7, local copies, waits for them, and re-layouts, scatter_sum(): kept = lax.dynamic_index_in_dim(values, mine, place, keepdims=False)  10.8 us
  transfers between devices with their start and end apart: 50, of which 28 were waited for; matrix products, arithmetic and copies ran while one was open for 18% of the time, Pallas kernels for 0%

profile of v1, /device:TPU:0, one launch (start us, length us, event | category | flops | bytes accessed | tf_op | source)
XLA Modules:
  0.0 515.1 jit_solution(15368842965431238511)
XLA Ops:
  14.1 3.0 collective-permute-start
  19.2 5.0 fusion.3
  25.4 116.1 %all-gather.2.cloned.1.call-done = bf16[768,12288]{1,0:T(8,128)(2,1)} async-done(((bf16[24,12288]{1,0:T(8,128)(2,1)}), bf16[768,12288]{1,0:T(8,128)(2,1)}) %all-gather.2.cloned.1.call-update) | async-done | bytes 18874384 | tf_op jit(solution)/shard_map/all_gather | solution.py:141
  141.5 3.6 convolution_convert_fusion
  147.3 4.1 fusion.15
  151.5 3.2 fusion.146
  154.6 2.5 copy.122
  157.2 2.7 convolution_convert_fusion.5
  162.7 8.2 %convolution_convert_fusion.15 = bf16[12,64,192]{2,1,0:T(8,128)(2,1)} fusion(bf16[384,12,64]{0,2,1:T(8,128)(2,1)} %bitcast.391, f32[12,192]{1,0:T(8,128)} %get-tuple-element.84, f32[12,192,384]{2,1,0:T(8,128)} %copy-done.4), kind=kOutput, calls=%fused_computation.105 | convolution fusion | flops 116050560 | bytes 4432896 | tf_op jit(solution)/shard_map/hrs,shd->rhd/dot_general | solution.py:47
  173.7 2.4 convolution_convert_fusion.18
  180.0 3.8 fusion.147
  183.8 3.2 convolution_convert_fusion.14
  189.2 4.4 fusion.6
  193.7 5.0 fusion.39
  198.7 6.1 %multiply_reduce_fusion.2 = (f32[768]{0:T(1024)S(1)}, f32[192]{0:T(256)S(1)}, f32[192,768]{1,0:T(8,128)S(1)}) fusion(f32[192,768]{1,0:T(8,128)S(1)} %get-tuple-element.91, f32[192]{0:T(256)S(1)} %fusion.128, f32[768]{0:T(1024)S(1)} %copy-done.74, bf16[768,12288]{1,0:T(8,128)(2,1)} %all-gather.2.cloned.1.call-done, ...), kind=kOutput, calls=%fused_computation.188 | convolution fusion | flops 1211988992 | bytes 9051648 | tf_op jit(solution)/shard_map/tk,ck->tc/dot_general | solution.py:227
  205.8 2.5 convolution_convert_fusion.17
  210.3 3.2 multiply_reduce_fusion.1
  215.9 2.5 multiply_reduce_fusion.3
  219.5 2.5 convolution_convert_fusion.16
  223.9 8.7 %fusion.148 = (bf16[384,12,64]{0,2,1:T(8,128)(2,1)}, f32[384,12,64]{0,2,1:T(8,128)}) fusion(bf16[192,12,64]{0,2,1:T(8,128)(2,1)} %bitcast.397, f32[12,192]{1,0:T(8,128)} %get-tuple-element.84, f32[12,192,384]{2,1,0:T(8,128)} %copy-done.4), kind=kOutput, calls=%fused_computation.325 | convolution fusion | flops 116198016 | bytes 5612544 | tf_op jit(solution)/shard_map/hrs,rhd->shd/dot_general | solution.py:58
  235.0 2.6 multiply_convert_fusion
  244.2 4.2 fusion.68
  253.1 2.7 convolution_convert_fusion.3
  290.0 4.0 fusion.65
  297.7 3.1 copy.144
  300.7 2.9 copy.198
  309.9 3.5 fusion.54
  315.1 3.5 fusion.97
  332.2 2.8 collective-permute-done.7
  347.7 3.4 collective-permute-done.10
  352.7 3.5 collective-permute-done.21
  356.5 5.7 %collective-permute-done.16 = bf16[2,2,24,768]{3,2,1,0:T(8,128)(2,1)S(1)} collective-permute-done((bf16[2,2,24,768]{3,2,1,0:T(8,128)(2,1)S(1)}, bf16[2,2,24,768]{3,2,1,0:T(8,128)(2,1)S(1)}, u32[]{:S(2)}, u32[]{:S(2)}) %collective-permute-start.16) | collective-permute-done | bytes 147488 | tf_op jit(solution)/shard_map/ppermute | solution.py:83
  363.8 7.2 %collective-permute-done.11 = bf16[2,2,24,768]{3,2,0,1:T(8,128)(2,1)S(1)} collective-permute-done((bf16[2,2,24,768]{3,2,0,1:T(8,128)(2,1)S(1)}, bf16[2,2,24,768]{3,2,0,1:T(8,128)(2,1)S(1)}, u32[]{:S(2)}, u32[]{:S(2)}) %collective-permute-start.11) | collective-permute-done | bytes 147488 | tf_op jit(solution)/shard_map/ppermute | solution.py:83
  371.0 4.3 collective-permute-done.22
  376.5 4.6 collective-permute-done.17
  382.8 2.7 collective-permute-done.12
  386.2 4.1 collective-permute-done.23
  407.4 9.6 %collective-permute-done.25 = bf16[2,2,2,24,1536]{4,3,2,1,0:T(8,128)(2,1)S(1)} collective-permute-done((bf16[2,2,2,24,1536]{4,3,2,1,0:T(8,128)(2,1)S(1)}, bf16[2,2,2,24,1536]{4,3,2,1,0:T(8,128)(2,1)S(1)}, u32[]{:S(2)}, u32[]{:S(2)}) %collective-permute-start.25) | collective-permute-done | bytes 589856 | tf_op jit(solution)/shard_map/ppermute | solution.py:83
  420.3 17.2 %collective-permute-done.26 = bf16[2,2,24,1536]{3,2,1,0:T(8,128)(2,1)S(1)} collective-permute-done((bf16[2,2,24,1536]{3,2,1,0:T(8,128)(2,1)S(1)}, bf16[2,2,24,1536]{3,2,1,0:T(8,128)(2,1)S(1)}, u32[]{:S(2)}, u32[]{:S(2)}) %collective-permute-start.26) | collective-permute-done | bytes 294944 | tf_op jit(solution)/shard_map/ppermute | solution.py:83
  445.7 2.9 collective-permute-done.28
  449.6 3.4 collective-permute-start.41
  455.7 12.2 %collective-permute-done.30 = bf16[2,2,2,24,2304]{4,3,2,0,1:T(8,128)(2,1)S(1)} collective-permute-done((bf16[2,2,2,24,2304]{4,3,2,0,1:T(8,128)(2,1)S(1)}, bf16[2,2,2,24,2304]{4,3,2,0,1:T(8,128)(2,1)S(1)}, u32[]{:S(2)}, u32[]{:S(2)}) %collective-permute-start.30) | collective-permute-done | bytes 884768 | tf_op jit(solution)/shard_map/ppermute | solution.py:83
  468.3 3.2 collective-permute-start.31
  475.1 3.2 collective-permute-start.47
  479.3 5.2 %collective-permute-done.37 = bf16[2,24,2048]{2,1,0:T(8,128)(2,1)S(1)} collective-permute-done((bf16[2,24,2048]{2,1,0:T(8,128)(2,1)S(1)}, bf16[2,24,2048]{2,1,0:T(8,128)(2,1)S(1)}, u32[]{:S(2)}, u32[]{:S(2)}) %collective-permute-start.37) | collective-permute-done | bytes 196640 | tf_op jit(solution)/shard_map/ppermute | solution.py:83
  490.1 2.8 collective-permute-start.32
  493.7 8.1 %collective-permute-done.32 = bf16[2,24,2304]{2,1,0:T(8,128)(2,1)S(1)} collective-permute-done((bf16[2,24,2304]{2,1,0:T(8,128)(2,1)S(1)}, bf16[2,24,2304]{2,1,0:T(8,128)(2,1)S(1)}, u32[]{:S(2)}, u32[]{:S(2)}) %collective-permute-start.32) | collective-permute-done | bytes 221216 | tf_op jit(solution)/shard_map/ppermute | solution.py:83
  502.7 4.0 collective-permute-done.33
  (435 shorter events, 170.0 us)
Async XLA Ops:
  7.2 134.3 %all-gather.2.cloned.1.call-start = ((), (), s32[]{:S(2)}) async-start(), calls=%async_computation | async-start | bytes 19464192 | tf_op jit(solution)/shard_map/all_gather | solution.py:141
  14.1 10.9 %collective-permute-start = (bf16[192,768]{1,0:T(8,128)(2,1)S(1)}, bf16[192,768]{1,0:T(8,128)(2,1)S(1)}, u32[]{:S(2)}, u32[]{:S(2)}) collective-permute-start(bf16[192,768]{1,0:T(8,128)(2,1)S(1)} %bitcast.360), channel_id=1, source_target_pairs={{0,1},{1,0},{2,3},{3,2},{4,5},{5,4},{6,7},{7,6},{8,9},{9,8},{10,11... | collective-permute-start | bytes 884744 | tf_op jit(solution)/shard_map/ppermute | solution.py:83
  17.2 140.0 %collective-permute-start.1 = (bf16[128,768]{1,0:T(8,128)(2,1)}, bf16[128,768]{1,0:T(8,128)(2,1)}, u32[]{:S(2)}, u32[]{:S(2)}) collective-permute-start(bf16[128,768]{1,0:T(8,128)(2,1)} %bitcast.10), channel_id=1, source_target_pairs={{0,1},{1,0},{2,3},{3,2},{4,5},{5,4},{6,7},{7,6},{8,9},{9,8},{10,11... | collective-permute-start | bytes 589832 | tf_op jit(solution)/shard_map/ppermute | solution.py:83
  265.3 48.1 %collective-permute-start.2 = (bf16[192,1536]{1,0:T(8,128)(2,1)}, bf16[192,1536]{1,0:T(8,128)(2,1)}, u32[]{:S(2)}, u32[]{:S(2)}) collective-permute-start(bf16[192,1536]{1,0:T(8,128)(2,1)} %pad_maximum_fusion.4), channel_id=1, source_target_pairs={{0,1},{1,0},{2,3},{3,2},{4,5},{5,4},{6,7},{7,6},{8,9},{9,8},{10,11... | collective-permute-start | bytes 1769480 | tf_op jit(solution)/shard_map/ppermute | solution.py:83
  269.0 40.3 %collective-permute-start.3 = (bf16[128,1536]{0,1:T(8,128)(2,1)}, bf16[128,1536]{0,1:T(8,128)(2,1)}, u32[]{:S(2)}, u32[]{:S(2)}) collective-permute-start(bf16[128,1536]{0,1:T(8,128)(2,1)} %slice.170), channel_id=1, source_target_pairs={{0,1},{1,0},{2,3},{3,2},{4,5},{5,4},{6,7},{7,6},{8,9},{9,8},{10,11... | collective-permute-start | bytes 1179656 | tf_op jit(solution)/shard_map/ppermute | solution.py:83
  272.2 46.5 %collective-permute-start.19 = (bf16[2,2,2,2,24,768]{5,4,0,1,2,3:T(8,128)(2,1)}, bf16[2,2,2,2,24,768]{5,4,0,1,2,3:T(8,128)(2,1)}, u32[]{:S(2)}, u32[]{:S(2)}) collective-permute-start(bf16[2,2,2,2,24,768]{5,4,0,1,2,3:T(8,128)(2,1)} %bitcast.345), channel_id=1, source_target_pairs={{0,2},{1,3},{2,0},{3,1},{4,6},{5,7},{6,4},{7,5},{8,10},{9,11},{10,... | collective-permute-start | bytes 1769480 | tf_op jit(solution)/shard_map/ppermute | solution.py:83
  274.8 46.4 %collective-permute-start.14 = (bf16[2,2,2,2,24,768]{5,4,3,0,1,2:T(8,128)(2,1)}, bf16[2,2,2,2,24,768]{5,4,3,0,1,2:T(8,128)(2,1)}, u32[]{:S(2)}, u32[]{:S(2)}) collective-permute-start(bf16[2,2,2,2,24,768]{5,4,3,0,1,2:T(8,128)(2,1)} %bitcast.346), channel_id=1, source_target_pairs={{0,2},{1,3},{2,0},{3,1},{4,6},{5,7},{6,4},{7,5},{8,10},{9,11},{10,... | collective-permute-start | bytes 1769480 | tf_op jit(solution)/shard_map/ppermute | solution.py:83
  277.6 50.0 %collective-permute-start.9 = (bf16[2,2,2,2,24,768]{5,4,2,3,0,1:T(8,128)(2,1)}, bf16[2,2,2,2,24,768]{5,4,2,3,0,1:T(8,128)(2,1)}, u32[]{:S(2)}, u32[]{:S(2)}) collective-permute-start(bf16[2,2,2,2,24,768]{5,4,2,3,0,1:T(8,128)(2,1)} %bitcast.347), channel_id=1, source_target_pairs={{0,2},{1,3},{2,0},{3,1},{4,6},{5,7},{6,4},{7,5},{8,10},{9,11},{10,... | collective-permute-start | bytes 1769480 | tf_op jit(solution)/shard_map/ppermute | solution.py:83
  309.3 89.7 %collective-permute-start.24 = (bf16[2,2,2,2,24,1536]{5,4,3,2,1,0:T(8,128)(2,1)}, bf16[2,2,2,2,24,1536]{5,4,3,2,1,0:T(8,128)(2,1)}, u32[]{:S(2)}, u32[]{:S(2)}) collective-permute-start(bf16[2,2,2,2,24,1536]{5,4,3,2,1,0:T(8,128)(2,1)} %dynamic-slice_bitcast_fusion), channel_id=1, source_target_pairs={{0,2},{1,3},{2,0},{3,1},{4,6},{5,7},{6,4},{7,5},{8,10},{9,11},{10,... | collective-permute-start | bytes 3538952 | tf_op jit(solution)/shard_map/ppermute | solution.py:83
  313.4 126.0 %collective-permute-start.29 = (bf16[2,2,2,2,24,2304]{5,4,3,0,1,2:T(8,128)(2,1)}, bf16[2,2,2,2,24,2304]{5,4,3,0,1,2:T(8,128)(2,1)}, u32[]{:S(2)}, u32[]{:S(2)}) collective-permute-start(bf16[2,2,2,2,24,2304]{5,4,3,0,1,2:T(8,128)(2,1)} %bitcast.341), channel_id=1, source_target_pairs={{0,2},{1,3},{2,0},{3,1},{4,6},{5,7},{6,4},{7,5},{8,10},{9,11},{10,... | collective-permute-start | bytes 5308424 | tf_op jit(solution)/shard_map/ppermute | solution.py:83
  318.7 82.2 %collective-permute-start.39 = (bf16[2,2,2,2,24,2048]{5,4,2,3,0,1:T(8,128)(2,1)}, bf16[2,2,2,2,24,2048]{5,4,2,3,0,1:T(8,128)(2,1)}, u32[]{:S(2)}, u32[]{:S(2)}) collective-permute-start(bf16[2,2,2,2,24,2048]{5,4,2,3,0,1:T(8,128)(2,1)} %bitcast.343), channel_id=1, source_target_pairs={{0,2},{1,3},{2,0},{3,1},{4,6},{5,7},{6,4},{7,5},{8,10},{9,11},{10,... | collective-permute-start | bytes 4718600 | tf_op jit(solution)/shard_map/ppermute | solution.py:83
  321.2 3.7 collective-permute-start.4
  326.1 18.1 %collective-permute-start.20 = (bf16[2,2,2,24,768]{4,3,0,1,2:T(8,128)(2,1)}, bf16[2,2,2,24,768]{4,3,0,1,2:T(8,128)(2,1)}, u32[]{:S(2)}, u32[]{:S(2)}) collective-permute-start(bf16[2,2,2,24,768]{4,3,0,1,2:T(8,128)(2,1)} %dynamic-slice_bitcast_fusion.11), channel_id=1, source_target_pairs={{0,1},{1,0},{2,3},{3,2},{4,5},{5,4},{6,7},{7,6},{8,9},{9,8},{10,11... | collective-permute-start | bytes 884744 | tf_op jit(solution)/shard_map/ppermute | solution.py:83
  327.6 3.7 collective-permute-start.6
  335.0 4.6 collective-permute-start.8
  339.6 7.0 %collective-permute-start.15 = (bf16[2,2,2,24,768]{4,3,2,0,1:T(8,128)(2,1)}, bf16[2,2,2,24,768]{4,3,2,0,1:T(8,128)(2,1)}, u32[]{:S(2)}, u32[]{:S(2)}) collective-permute-start(bf16[2,2,2,24,768]{4,3,2,0,1:T(8,128)(2,1)} %dynamic-slice_bitcast_fusion.12), channel_id=1, source_target_pairs={{0,4},{1,5},{2,6},{3,7},{4,0},{5,1},{6,2},{7,3},{8,12},{9,13},{10,... | collective-permute-start | bytes 884744 | tf_op jit(solution)/shard_map/ppermute | solution.py:83
  344.2 6.9 %collective-permute-start.10 = (bf16[2,2,2,24,768]{4,3,1,2,0:T(8,128)(2,1)}, bf16[2,2,2,24,768]{4,3,1,2,0:T(8,128)(2,1)S(1)}, u32[]{:S(2)}, u32[]{:S(2)}) collective-permute-start(bf16[2,2,2,24,768]{4,3,1,2,0:T(8,128)(2,1)} %dynamic-slice_bitcast_fusion.13), channel_id=1, source_target_pairs={{0,8},{1,9},{2,10},{3,11},{4,12},{5,13},{6,14},{7,15},{8,0},{9,1},... | collective-permute-start | bytes 884744 | tf_op jit(solution)/shard_map/ppermute | solution.py:83
  346.6 58.3 %collective-permute-start.34 = (bf16[2,2,2,2,24,2048]{5,4,3,0,1,2:T(8,128)(2,1)}, bf16[2,2,2,2,24,2048]{5,4,3,0,1,2:T(8,128)(2,1)S(1)}, u32[]{:S(2)}, u32[]{:S(2)}) collective-permute-start(bf16[2,2,2,2,24,2048]{5,4,3,0,1,2:T(8,128)(2,1)} %bitcast.384), channel_id=1, source_target_pairs={{0,2},{1,3},{2,0},{3,1},{4,6},{5,7},{6,4},{7,5},{8,10},{9,11},{10,... | collective-permute-start | bytes 4718600 | tf_op jit(solution)/shard_map/ppermute | solution.py:83
  351.1 5.1 collective-permute-start.21
  356.3 5.9 %collective-permute-start.16 = (bf16[2,2,24,768]{3,2,1,0:T(8,128)(2,1)S(1)}, bf16[2,2,24,768]{3,2,1,0:T(8,128)(2,1)S(1)}, u32[]{:S(2)}, u32[]{:S(2)}) collective-permute-start(bf16[2,2,24,768]{3,2,1,0:T(8,128)(2,1)S(1)} %dynamic-slice_bitcast_fusion.20), channel_id=1, source_target_pairs={{0,8},{1,9},{2,10},{3,11},{4,12},{5,13},{6,14},{7,15},{8,0},{9,1},... | collective-permute-start | bytes 442376 | tf_op jit(solution)/shard_map/ppermute | solution.py:83
  362.2 8.7 %collective-permute-start.11 = (bf16[2,2,24,768]{3,2,0,1:T(8,128)(2,1)S(1)}, bf16[2,2,24,768]{3,2,0,1:T(8,128)(2,1)S(1)}, u32[]{:S(2)}, u32[]{:S(2)}) collective-permute-start(bf16[2,2,24,768]{3,2,0,1:T(8,128)(2,1)S(1)} %dynamic-slice_bitcast_fusion.21), channel_id=1, source_target_pairs={{0,16},{1,17},{2,18},{3,19},{4,20},{5,21},{6,22},{7,23},{8,24},{9,... | collective-permute-start | bytes 442376 | tf_op jit(solution)/shard_map/ppermute | solution.py:83
  370.9 4.4 collective-permute-start.22
  375.3 5.8 %collective-permute-start.17 = (bf16[2,24,768]{2,1,0:T(8,128)(2,1)S(1)}, bf16[2,24,768]{2,1,0:T(8,128)(2,1)S(1)}, u32[]{:S(2)}, u32[]{:S(2)}) collective-permute-start(bf16[2,24,768]{2,1,0:T(8,128)(2,1)S(1)} %dynamic-slice_bitcast_fusion.28), channel_id=1, source_target_pairs={{0,16},{1,17},{2,18},{3,19},{4,20},{5,21},{6,22},{7,23},{8,24},{9,... | collective-permute-start | bytes 221192 | tf_op jit(solution)/shard_map/ppermute | solution.py:83
  381.1 4.4 collective-permute-start.12
  385.5 4.9 collective-permute-start.23
  390.3 4.0 collective-permute-start.18
  394.3 4.0 collective-permute-start.13
  398.2 20.0 %collective-permute-start.44 = (bf16[2,2,2,2,24,2048]{5,4,0,1,2,3:T(8,128)(2,1)S(1)}, bf16[2,2,2,2,24,2048]{5,4,0,1,2,3:T(8,128)(2,1)S(1)}, u32[]{:S(2)}, u32[]{:S(2)}) collective-permute-start(bf16[2,2,2,2,24,2048]{5,4,0,1,2,3:T(8,128)(2,1)S(1)} %bitcast.383), channel_id=1, source_target_pairs={{0,2},{1,3},{2,0},{3,1},{4,6},{5,7},{6,4},{7,5},{8,10},{9,11},{10,... | collective-permute-start | bytes 4718600 | tf_op jit(solution)/shard_map/ppermute | solution.py:83
  400.8 16.2 %collective-permute-start.25 = (bf16[2,2,2,24,1536]{4,3,2,1,0:T(8,128)(2,1)S(1)}, bf16[2,2,2,24,1536]{4,3,2,1,0:T(8,128)(2,1)S(1)}, u32[]{:S(2)}, u32[]{:S(2)}) collective-permute-start(bf16[2,2,2,24,1536]{4,3,2,1,0:T(8,128)(2,1)S(1)} %dynamic-slice_bitcast_fusion.5), channel_id=1, source_target_pairs={{0,8},{1,9},{2,10},{3,11},{4,12},{5,13},{6,14},{7,15},{8,0},{9,1},... | collective-permute-start | bytes 1769480 | tf_op jit(solution)/shard_map/ppermute | solution.py:83
  402.8 46.4 %collective-permute-start.40 = (bf16[2,2,2,24,2048]{4,3,1,2,0:T(8,128)(2,1)S(1)}, bf16[2,2,2,24,2048]{4,3,1,2,0:T(8,128)(2,1)S(1)}, u32[]{:S(2)}, u32[]{:S(2)}) collective-permute-start(bf16[2,2,2,24,2048]{4,3,1,2,0:T(8,128)(2,1)S(1)} %dynamic-slice_bitcast_fusion.3), channel_id=1, source_target_pairs={{0,8},{1,9},{2,10},{3,11},{4,12},{5,13},{6,14},{7,15},{8,0},{9,1},... | collective-permute-start | bytes 2359304 | tf_op jit(solution)/shard_map/ppermute | solution.py:83
  405.6 47.4 %collective-permute-start.35 = (bf16[2,2,2,24,2048]{4,3,2,0,1:T(8,128)(2,1)S(1)}, bf16[2,2,2,24,2048]{4,3,2,0,1:T(8,128)(2,1)S(1)}, u32[]{:S(2)}, u32[]{:S(2)}) collective-permute-start(bf16[2,2,2,24,2048]{4,3,2,0,1:T(8,128)(2,1)S(1)} %dynamic-slice_bitcast_fusion.4), channel_id=1, source_target_pairs={{0,4},{1,5},{2,6},{3,7},{4,0},{5,1},{6,2},{7,3},{8,12},{9,13},{10,... | collective-permute-start | bytes 2359304 | tf_op jit(solution)/shard_map/ppermute | solution.py:83
  417.2 20.4 %collective-permute-start.26 = (bf16[2,2,24,1536]{3,2,1,0:T(8,128)(2,1)S(1)}, bf16[2,2,24,1536]{3,2,1,0:T(8,128)(2,1)S(1)}, u32[]{:S(2)}, u32[]{:S(2)}) collective-permute-start(bf16[2,2,24,1536]{3,2,1,0:T(8,128)(2,1)S(1)} %dynamic-slice_bitcast_fusion.10), channel_id=1, source_target_pairs={{0,16},{1,17},{2,18},{3,19},{4,20},{5,21},{6,22},{7,23},{8,24},{9,... | collective-permute-start | bytes 884744 | tf_op jit(solution)/shard_map/ppermute | solution.py:83
  418.9 34.6 %collective-permute-start.45 = (bf16[2,2,2,24,2048]{4,3,0,1,2:T(8,128)(2,1)S(1)}, bf16[2,2,2,24,2048]{4,3,0,1,2:T(8,128)(2,1)S(1)}, u32[]{:S(2)}, u32[]{:S(2)}) collective-permute-start(bf16[2,2,2,24,2048]{4,3,0,1,2:T(8,128)(2,1)S(1)} %dynamic-slice_bitcast_fusion.2), channel_id=1, source_target_pairs={{0,1},{1,0},{2,3},{3,2},{4,5},{5,4},{6,7},{7,6},{8,9},{9,8},{10,11... | collective-permute-start | bytes 2359304 | tf_op jit(solution)/shard_map/ppermute | solution.py:83
  437.7 5.7 %collective-permute-start.27 = (bf16[2,24,1536]{2,1,0:T(8,128)(2,1)S(1)}, bf16[2,24,1536]{2,1,0:T(8,128)(2,1)S(1)}, u32[]{:S(2)}, u32[]{:S(2)}) collective-permute-start(bf16[2,24,1536]{2,1,0:T(8,128)(2,1)S(1)} %dynamic-slice_bitcast_fusion.18), channel_id=1, source_target_pairs={{0,1},{1,0},{2,3},{3,2},{4,5},{5,4},{6,7},{7,6},{8,9},{9,8},{10,11... | collective-permute-start | bytes 442376 | tf_op jit(solution)/shard_map/ppermute | solution.py:83
  443.5 5.1 collective-permute-start.28
  445.3 22.6 %collective-permute-start.30 = (bf16[2,2,2,24,2304]{4,3,2,0,1:T(8,128)(2,1)S(1)}, bf16[2,2,2,24,2304]{4,3,2,0,1:T(8,128)(2,1)S(1)}, u32[]{:S(2)}, u32[]{:S(2)}) collective-permute-start(bf16[2,2,2,24,2304]{4,3,2,0,1:T(8,128)(2,1)S(1)} %dynamic-slice_bitcast_fusion.1), channel_id=1, source_target_pairs={{0,4},{1,5},{2,6},{3,7},{4,0},{5,1},{6,2},{7,3},{8,12},{9,13},{10,... | collective-permute-start | bytes 2654216 | tf_op jit(solution)/shard_map/ppermute | solution.py:83
  449.6 21.8 %collective-permute-start.41 = (bf16[2,2,24,2048]{3,2,0,1:T(8,128)(2,1)S(1)}, bf16[2,2,24,2048]{3,2,0,1:T(8,128)(2,1)S(1)}, u32[]{:S(2)}, u32[]{:S(2)}) collective-permute-start(bf16[2,2,24,2048]{3,2,0,1:T(8,128)(2,1)S(1)} %dynamic-slice_bitcast_fusion.8), channel_id=1, source_target_pairs={{0,16},{1,17},{2,18},{3,19},{4,20},{5,21},{6,22},{7,23},{8,24},{9,... | collective-permute-start | bytes 1179656 | tf_op jit(solution)/shard_map/ppermute | solution.py:83
  453.4 19.6 %collective-permute-start.36 = (bf16[2,2,24,2048]{3,2,1,0:T(8,128)(2,1)S(1)}, bf16[2,2,24,2048]{3,2,1,0:T(8,128)(2,1)S(1)}, u32[]{:S(2)}, u32[]{:S(2)}) collective-permute-start(bf16[2,2,24,2048]{3,2,1,0:T(8,128)(2,1)S(1)} %dynamic-slice_bitcast_fusion.9), channel_id=1, source_target_pairs={{0,8},{1,9},{2,10},{3,11},{4,12},{5,13},{6,14},{7,15},{8,0},{9,1},... | collective-permute-start | bytes 1179656 | tf_op jit(solution)/shard_map/ppermute | solution.py:83
  453.8 21.1 %collective-permute-start.46 = (bf16[2,2,24,2048]{3,2,0,1:T(8,128)(2,1)S(1)}, bf16[2,2,24,2048]{3,2,0,1:T(8,128)(2,1)S(1)}, u32[]{:S(2)}, u32[]{:S(2)}) collective-permute-start(bf16[2,2,24,2048]{3,2,0,1:T(8,128)(2,1)S(1)} %dynamic-slice_bitcast_fusion.7), channel_id=1, source_target_pairs={{0,4},{1,5},{2,6},{3,7},{4,0},{5,1},{6,2},{7,3},{8,12},{9,13},{10,... | collective-permute-start | bytes 1179656 | tf_op jit(solution)/shard_map/ppermute | solution.py:83
  468.3 21.7 %collective-permute-start.31 = (bf16[2,2,24,2304]{3,2,1,0:T(8,128)(2,1)S(1)}, bf16[2,2,24,2304]{3,2,1,0:T(8,128)(2,1)S(1)}, u32[]{:S(2)}, u32[]{:S(2)}) collective-permute-start(bf16[2,2,24,2304]{3,2,1,0:T(8,128)(2,1)S(1)} %dynamic-slice_bitcast_fusion.6), channel_id=1, source_target_pairs={{0,8},{1,9},{2,10},{3,11},{4,12},{5,13},{6,14},{7,15},{8,0},{9,1},... | collective-permute-start | bytes 1327112 | tf_op jit(solution)/shard_map/ppermute | solution.py:83
  471.5 6.7 %collective-permute-start.42 = (bf16[2,24,2048]{2,1,0:T(8,128)(2,1)S(1)}, bf16[2,24,2048]{2,1,0:T(8,128)(2,1)S(1)}, u32[]{:S(2)}, u32[]{:S(2)}) collective-permute-start(bf16[2,24,2048]{2,1,0:T(8,128)(2,1)S(1)} %dynamic-slice_bitcast_fusion.16), channel_id=1, source_target_pairs={{0,1},{1,0},{2,3},{3,2},{4,5},{5,4},{6,7},{7,6},{8,9},{9,8},{10,11... | collective-permute-start | bytes 589832 | tf_op jit(solution)/shard_map/ppermute | solution.py:83
  473.1 11.4 %collective-permute-start.37 = (bf16[2,24,2048]{2,1,0:T(8,128)(2,1)S(1)}, bf16[2,24,2048]{2,1,0:T(8,128)(2,1)S(1)}, u32[]{:S(2)}, u32[]{:S(2)}) collective-permute-start(bf16[2,24,2048]{2,1,0:T(8,128)(2,1)S(1)} %dynamic-slice_bitcast_fusion.17), channel_id=1, source_target_pairs={{0,16},{1,17},{2,18},{3,19},{4,20},{5,21},{6,22},{7,23},{8,24},{9,... | collective-permute-start | bytes 589832 | tf_op jit(solution)/shard_map/ppermute | solution.py:83
  475.1 12.3 %collective-permute-start.47 = (bf16[2,24,2048]{2,1,0:T(8,128)(2,1)S(1)}, bf16[2,24,2048]{2,1,0:T(8,128)(2,1)S(1)}, u32[]{:S(2)}, u32[]{:S(2)}) collective-permute-start(bf16[2,24,2048]{2,1,0:T(8,128)(2,1)S(1)} %dynamic-slice_bitcast_fusion.15), channel_id=1, source_target_pairs={{0,8},{1,9},{2,10},{3,11},{4,12},{5,13},{6,14},{7,15},{8,0},{9,1},... | collective-permute-start | bytes 589832 | tf_op jit(solution)/shard_map/ppermute | solution.py:83
  478.3 11.6 %collective-permute-start.43 = (bf16[24,2048]{1,0:T(8,128)(2,1)S(1)}, bf16[24,2048]{1,0:T(8,128)(2,1)S(1)}, u32[]{:S(2)}, u32[]{:S(2)}) collective-permute-start(bf16[24,2048]{1,0:T(8,128)(2,1)S(1)} %dynamic-slice_bitcast_fusion.24), channel_id=1, source_target_pairs={{0,4},{1,5},{2,6},{3,7},{4,0},{5,1},{6,2},{7,3},{8,12},{9,13},{10,... | collective-permute-start | bytes 294920 | tf_op jit(solution)/shard_map/ppermute | solution.py:83
  484.6 5.3 %collective-permute-start.38 = (bf16[24,2048]{1,0:T(8,128)(2,1)S(1)}, bf16[24,2048]{1,0:T(8,128)(2,1)S(1)}, u32[]{:S(2)}, u32[]{:S(2)}) collective-permute-start(bf16[24,2048]{1,0:T(8,128)(2,1)S(1)} %dynamic-slice_bitcast_fusion.25), channel_id=1, source_target_pairs={{0,1},{1,0},{2,3},{3,2},{4,5},{5,4},{6,7},{7,6},{8,9},{9,8},{10,11... | collective-permute-start | bytes 294920 | tf_op jit(solution)/shard_map/ppermute | solution.py:83
  487.4 14.5 %collective-permute-start.48 = (bf16[24,2048]{1,0:T(8,128)(2,1)S(1)}, bf16[24,2048]{1,0:T(8,128)(2,1)S(1)}, u32[]{:S(2)}, u32[]{:S(2)}) collective-permute-start(bf16[24,2048]{1,0:T(8,128)(2,1)S(1)} %dynamic-slice_bitcast_fusion.23), channel_id=1, source_target_pairs={{0,16},{1,17},{2,18},{3,19},{4,20},{5,21},{6,22},{7,23},{8,24},{9,... | collective-permute-start | bytes 294920 | tf_op jit(solution)/shard_map/ppermute | solution.py:83
  490.1 11.7 %collective-permute-start.32 = (bf16[2,24,2304]{2,1,0:T(8,128)(2,1)S(1)}, bf16[2,24,2304]{2,1,0:T(8,128)(2,1)S(1)}, u32[]{:S(2)}, u32[]{:S(2)}) collective-permute-start(bf16[2,24,2304]{2,1,0:T(8,128)(2,1)S(1)} %dynamic-slice_bitcast_fusion.14), channel_id=1, source_target_pairs={{0,16},{1,17},{2,18},{3,19},{4,20},{5,21},{6,22},{7,23},{8,24},{9,... | collective-permute-start | bytes 663560 | tf_op jit(solution)/shard_map/ppermute | solution.py:83
  501.9 4.8 collective-permute-start.33
  (93 other events, 592.8 us)
Sparse Core Ops, SparseCore 0:
  14.3 127.2 all-gather.1

commit v2 on v1

--- a/solution.py
+++ b/solution.py
@@ -89,25 +89,54 @@
     return [1] + rest[turn:] + rest[:turn]
 
 
-def scatter_sum(values, order, devices, index):
-    bits = len(order)
-    values = values.reshape((2,) * bits + (values.shape[0] // devices, values.shape[1]))
-    left = list(range(bits - 1, -1, -1))
-    for bit in order:
-        place = left.index(bit)
-        mine = (index >> bit) & 1
-        kept = lax.dynamic_index_in_dim(values, mine, place, keepdims=False)
-        sent = lax.dynamic_index_in_dim(values, 1 - mine, place, keepdims=False)
-        total = kept.astype(jnp.float32) + swap_bit(sent, bit, devices).astype(jnp.float32)
-        left.remove(bit)
-        values = total.astype(jnp.bfloat16) if left else total
-    return values
-
-
-def full_sum(values, bits, devices):
-    for bit in range(bits):
-        values = values + swap_bit(values, bit, devices)
-    return values
+def after(never, values, others):
+    first = [other[(0,) * other.ndim].astype(jnp.float32) for other in others]
+    return jnp.where(never, sum(first).astype(values.dtype), values)
+
+
+class HalvingSum:
+
+    def __init__(self, groups, devices, index, never, whole=None):
+        self.devices, self.index, self.never, self.whole = devices, index, never, whole
+        self.bits = devices.bit_length() - 1
+        self.at = 0
+        self.orders = [bit_order(self.bits, turn) for turn in range(len(groups))]
+        self.left = [list(range(self.bits - 1, -1, -1)) for group in groups]
+        self.groups = [
+            group.reshape((2,) * self.bits + (group.shape[0] // devices, group.shape[1]))
+            for group in groups
+        ]
+        self.sent = self.halves(1)
+
+    def halves(self, other):
+        found = []
+        for order, left, group in zip(self.orders, self.left, self.groups):
+            bit = order[self.at]
+            mine = ((self.index >> bit) & 1) ^ other
+            found.append(
+                lax.dynamic_index_in_dim(group, mine, left.index(bit), keepdims=False)
+            )
+        return found
+
+    def exchange(self):
+        kept = self.halves(0)
+        last = self.at == self.bits - 1
+        came = []
+        for order, left, sent in zip(self.orders, self.left, self.sent):
+            left.remove(order[self.at])
+            came.append(swap_bit(sent, order[self.at], self.devices))
+        if self.whole is not None:
+            self.whole = self.whole + swap_bit(
+                after(self.never, self.whole, self.sent[:1]), self.at, self.devices
+            )
+        totals = [one.astype(jnp.float32) + two.astype(jnp.float32) for one, two in zip(kept, came)]
+        self.at += 1
+        if last:
+            self.groups = totals
+            return
+        self.groups = [total.astype(jnp.bfloat16) for total in totals]
+        marks = came + ([] if self.whole is None else [self.whole])
+        self.sent = [after(self.never, sent, marks) for sent in self.halves(1)]
 
 
 def local(
@@ -134,8 +163,7 @@
     my_seq = lax.axis_index("seq")
     index = lax.axis_index("dp") * 2 + my_seq
 
-    def scattered(values, turn):
-        return scatter_sum(values, bit_order(bits, turn), devices, index)
+    never = segment_ids[0, 0] < 0
 
     shards = (attn_in, attn_out, cross_query, cross_kv, cross_out, ff_in, ff_out)
     gathered = lax.all_gather(jnp.concatenate(shards, 1), axes, axis=0, tiled=True)
@@ -213,7 +241,6 @@
     )
     grad_out = cotangent[0].astype(jnp.float32)
     grad_branch = cotangent[0]
-    ff_out_grad = scattered(outer_rows(grad_branch, mixed_act), 0)
     grad_mixed = jnp.einsum(
         "td,df->tf", grad_branch, ff_out_all, preferred_element_type=jnp.float32
     )
@@ -221,14 +248,24 @@
     grad_gate, grad_up = gate_pull(grad_mixed)
     grad_gate = grad_gate.astype(jnp.bfloat16)
     grad_up = grad_up.astype(jnp.bfloat16)
-    gate_grad = scattered(outer_rows(normed_three, grad_gate), 1)
-    up_grad = scattered(outer_rows(normed_three, grad_up), 2)
-    grad_pre = jnp.concatenate([grad_gate, grad_up], 1)
+    wave = HalvingSum(
+        [
+            outer_rows(grad_branch, mixed_act),
+            outer_rows(normed_three, grad_gate),
+            outer_rows(normed_three, grad_up),
+        ],
+        devices,
+        index,
+        never,
+    )
+    grad_pre = after(never, jnp.concatenate([grad_gate, grad_up], 1), wave.sent)
+    wave.exchange()
     grad_normed = jnp.einsum("tk,ck->tc", grad_pre, ff_in_all, preferred_element_type=jnp.float32)
     norm_value, norm_pull = jax.vjp(rms_scaled, hidden_two, norm_gains[2])
     grad_resid, gain_three = norm_pull(grad_normed)
     grad_hidden_two = grad_out + grad_resid
-    grad_branch_two = grad_hidden_two.astype(jnp.bfloat16)
+    grad_branch_two = after(never, grad_hidden_two.astype(jnp.bfloat16), wave.sent)
+    wave.exchange()
     grad_context_two = jnp.einsum(
         "tk,ck->tc", grad_branch_two, cross_out_all, preferred_element_type=jnp.float32
     )
@@ -244,17 +281,16 @@
         1,
     )
     kv_two_low = grad_kv_two.astype(jnp.bfloat16)
-    cross_grads = scattered(
-        jnp.concatenate(
-            [outer_rows(enc_both, kv_two_low), outer_rows(context_two, grad_branch_two)], 1
-        ),
-        1,
+    cross_grads = jnp.concatenate(
+        [outer_rows(enc_both, kv_two_low), outer_rows(context_two, grad_branch_two)], 1
     )
     grad_kv_local = (
         grad_kv_two[:enc_count]
         + swap_bit(kv_two_low[enc_count:], 0, devices).astype(jnp.float32)
     ).astype(jnp.bfloat16)
     grad_queries_two = grad_queries.reshape(tok_count, model_width).astype(jnp.bfloat16)
+    grad_queries_two = after(never, grad_queries_two, wave.sent)
+    wave.exchange()
     encoder_grad = jnp.einsum(
         "tk,ck->tc", grad_kv_local, cross_kv_all, preferred_element_type=jnp.float32
     )
@@ -265,16 +301,15 @@
     grad_resid, gain_two = norm_pull(grad_normed)
     grad_hidden_one = grad_hidden_two + grad_resid
     grad_branch_one = grad_hidden_one.astype(jnp.bfloat16)
-    middle_grads = scattered(
-        jnp.concatenate(
-            [outer_rows(normed_two, grad_queries_two), outer_rows(context_one, grad_branch_one)], 1
-        ),
-        2,
+    middle_grads = jnp.concatenate(
+        [outer_rows(normed_two, grad_queries_two), outer_rows(context_one, grad_branch_one)], 1
     )
     grad_context_one = jnp.einsum(
         "tk,ck->tc", grad_branch_one, attn_out_all, preferred_element_type=jnp.float32
     )
-    grad_context_one = grad_context_one.astype(jnp.bfloat16).reshape(tok_count, H, HD)
+    grad_context_one = after(never, grad_context_one.astype(jnp.bfloat16), wave.sent)
+    grad_context_one = grad_context_one.reshape(tok_count, H, HD)
+    wave.exchange()
     grad_queries, grad_keys, grad_values, grad_scores = attend_backward(
         queries_one, keys_one, values_one, weights_one, grad_context_one
     )
@@ -283,11 +318,16 @@
     keys_low = grad_keys.astype(jnp.bfloat16)
     values_low = grad_values.astype(jnp.bfloat16)
     grad_queries_one = grad_queries.reshape(tok_count, model_width).astype(jnp.bfloat16)
-    in_grads = [
-        scattered(outer_rows(normed_both, values_low), 0),
-        scattered(outer_rows(normed_both, keys_low), 1),
-        scattered(outer_rows(normed_both[:tok_count], grad_queries_one), 2),
-    ]
+    in_grads = jnp.concatenate(
+        [
+            outer_rows(normed_both[:tok_count], grad_queries_one),
+            outer_rows(normed_both, jnp.concatenate([keys_low, values_low], 1)),
+        ],
+        1,
+    )
+    while wave.at < bits:
+        wave.exchange()
+    ff_out_grad, gate_grad, up_grad = wave.groups
     other_part = swap_bit(
         jnp.concatenate([keys_low[tok_count:], values_low[tok_count:]], 1), 0, devices
     ).astype(jnp.float32)
@@ -303,14 +343,18 @@
     grad_resid, gain_one = norm_pull(grad_normed)
     tokens_grad = grad_hidden_one + grad_resid
     small = jnp.concatenate([gain_one, gain_two, gain_three, table_grad.reshape(-1)])
-    small = full_sum(small, bits, devices)
+    wave = HalvingSum([in_grads, cross_grads, middle_grads], devices, index, never, small)
+    for at in range(bits):
+        wave.exchange()
+    in_grads, cross_grads, middle_grads = wave.groups
+    small = wave.whole
     return (
         layer_out.astype(jnp.bfloat16)[None],
         tokens_grad[None],
         encoder_grad[None],
         small[: 3 * model_width].reshape(3, model_width),
         small[3 * model_width :].reshape(rel_table.shape),
-        jnp.concatenate([in_grads[2], in_grads[1], in_grads[0]], 1),
+        in_grads,
         middle_grads[:, model_width:],
         middle_grads[:, :model_width],
         cross_grads[:, : 2 * model_width],

time: 522 us -> 530 us (1.015)
  waiting for transfers between devices: 232 us -> 167 us
  local copies, waits for them, and re-layouts: 71.7 us -> 110 us
  between operations: 15.7 us -> 45.9 us
  other arithmetic: 33.2 us -> 54.1 us
  starting transfers between devices: 53.3 us -> 40.4 us
    ppermute x49 -> x39, waiting for transfers between devices: 116 us -> 56 us  [swap_bit(): lax.ppermute(values, axes, [(at, at ^ 1 << bit) for at in range(devices)])]
    slice x0 -> x46, local copies, waits for them, and re-layouts: none -> 47.2 us  [the longest x45 46.1 us: after(): first = [other[(0,) * other.ndim].astype(jnp.float32) for other in others]]
    select_n x0 -> x28, other arithmetic: none -> 12.9 us  [after(): return jnp.where(never, sum(first).astype(values.dtype), values)]
    ppermute x49 -> x39, starting transfers between devices: 53.2 us -> 40.4 us  [swap_bit(): lax.ppermute(values, axes, [(at, at ^ 1 << bit) for at in range(devices)])]
    convert_element_type x32 -> x23, other arithmetic: 14.8 us -> 24.2 us  [the longest x22 23.1 us: exchange(): self.groups = [total.astype(jnp.bfloat16) for total in totals]]
    dynamic_slice x14 -> x10, local copies, waits for them, and re-layouts: 20 us -> 14.5 us  [halves(): lax.dynamic_index_in_dim(group, mine, left.index(bit), keepdims=False)]
    dot_general x10 -> x9, matrix products: 13.4 us -> 9.37 us  [outer_rows(): jnp.einsum('tc,tk->ck', left, right, preferred_element_type=jnp.float32)]
    unnamed x189 -> x227, local copies, waits for them, and re-layouts: 15.6 us -> 16.4 us
  transfers between devices with their start and end apart: 50 -> 40, of which waited for: 28 -> 15; matrix products, arithmetic and copies ran while one was open for 18% -> 36% of each run, Pallas kernels for 0% -> 0%
where the time goes in v2:
time: 530 us; the launch traced here: 521 us
  waiting for transfers between devices  167 us (32%)
  local copies, waits for them, and re-layouts  110 us (21%)
  matrix products  104 us (20%)
  other arithmetic  54.1 us (10%)
  between operations  45.9 us (9%)
  starting transfers between devices  40.4 us (8%)
    all_gather x1, waiting for transfers between devices, local(): lax.all_gather(jnp.concatenate(shards, 1), axes, axis=0, tiled=True)  111 us
    ppermute x39, waiting for transfers between devices, swap_bit(): lax.ppermute(values, axes, [(at, at ^ 1 << bit) for at in range(devices)])  56 us
    slice x45, local copies, waits for them, and re-layouts, after(): first = [other[(0,) * other.ndim].astype(jnp.float32) for other in others]  46.1 us
    ppermute x39, starting transfers between devices, swap_bit(): lax.ppermute(values, axes, [(at, at ^ 1 << bit) for at in range(devices)])  40.4 us
    convert_element_type x22, other arithmetic, exchange(): self.groups = [total.astype(jnp.bfloat16) for total in totals]  23.1 us
    unnamed x227, local copies, waits for them, and re-layouts  16.4 us
    dynamic_slice x10, local copies, waits for them, and re-layouts, halves(): lax.dynamic_index_in_dim(group, mine, left.index(bit), keepdims=False)  14.5 us
    select_n x28, other arithmetic, after(): return jnp.where(never, sum(first).astype(values.dtype), values)  12.9 us
  transfers between devices with their start and end apart: 40, of which 15 were waited for; matrix products, arithmetic and copies ran while one was open for 36% of the time, Pallas kernels for 0%

profile of v2, /device:TPU:0, one launch (start us, length us, event | category | flops | bytes accessed | tf_op | source)
XLA Modules:
  0.0 521.0 jit_solution(6302609275654699924)
XLA Ops:
  14.2 3.0 collective-permute-start.1
  19.3 5.0 fusion.3
  24.3 5.7 %collective-permute-done = bf16[192,768]{1,0:T(8,128)(2,1)S(1)} collective-permute-done((bf16[192,768]{1,0:T(8,128)(2,1)S(1)}, bf16[192,768]{1,0:T(8,128)(2,1)S(1)}, u32[]{:S(2)}, u32[]{:S(2)}) %collective-permute-start) | collective-permute-done | bytes 294944 | tf_op jit(solution)/shard_map/ppermute | solution.py:83
  30.5 111.1 %all-gather.2.cloned.1.call-done = bf16[768,12288]{1,0:T(8,128)(2,1)} async-done(((bf16[24,12288]{1,0:T(8,128)(2,1)}), bf16[768,12288]{1,0:T(8,128)(2,1)}) %all-gather.2.cloned.1.call-update) | async-done | bytes 18874384 | tf_op jit(solution)/shard_map/all_gather | solution.py:169
  141.6 3.6 convolution_convert_fusion
  145.3 2.5 convolution_convert_fusion.6
  151.3 4.1 fusion.16
  155.4 3.2 fusion.148
  158.6 8.2 %convolution_convert_fusion.14 = bf16[12,64,192]{2,1,0:T(8,128)(2,1)} fusion(bf16[384,12,64]{0,2,1:T(8,128)(2,1)} %bitcast.368, f32[12,192]{1,0:T(8,128)} %get-tuple-element.82, f32[12,192,384]{2,1,0:T(8,128)} %copy-done.2), kind=kOutput, calls=%fused_computation.112 | convolution fusion | flops 116050560 | bytes 4432896 | tf_op jit(solution)/shard_map/hrs,shd->rhd/dot_general | solution.py:47
  166.8 2.0 multiply_reduce_fusion.7
  169.7 2.5 convolution_convert_fusion.17
  172.1 1.9 copy.158
  174.0 3.9 fusion.149
  177.9 3.2 convolution_convert_fusion.13
  181.1 2.1 multiply_reduce_fusion.6
  184.1 4.3 fusion.6
  188.4 4.1 fusion.40
  213.0 5.9 %multiply_reduce_fusion.2 = (f32[768]{0:T(1024)S(1)}, f32[192]{0:T(256)S(1)}, f32[192,768]{1,0:T(8,128)S(1)}) fusion(f32[192,768]{1,0:T(8,128)} %copy-done.18, f32[192]{0:T(256)} %copy-done.97, f32[768]{0:T(1024)S(1)} %copy-done.89, bf16[768,12288]{1,0:T(8,128)(2,1)} %all-gather.2.cloned.1.call-done, bf16[192,2048]{1,0:T(8,128)(2,1)} %copy-done.73, ...), kind=kOutput, calls=%fused_computation.189 | convolution fusion | flops 1212775424 | bytes 9052928 | tf_op jit(solution)/shard_map/tk,ck->tc/dot_general | solution.py:263
  220.0 4.1 fusion.67
  229.6 1.9 fusion.18
  248.0 2.5 convolution_convert_fusion.16
  250.5 1.9 copy.172
  252.4 3.3 fusion.105
  255.7 3.2 multiply_reduce_fusion.1
  266.9 5.2 collective-permute-done.12
  272.0 3.3 fusion.55
  300.2 2.6 multiply_reduce_fusion.3
  305.9 4.4 copy.185
  310.3 2.5 copy_bitcast_fusion.10
  331.8 2.6 fusion.66
  334.4 1.9 copy.173
  336.3 8.7 %fusion.150 = (bf16[384,12,64]{0,2,1:T(8,128)(2,1)}, f32[384,12,64]{0,2,1:T(8,128)}) fusion(bf16[192,12,64]{0,2,1:T(8,128)(2,1)} %bitcast.372, f32[12,192]{1,0:T(8,128)} %get-tuple-element.82, f32[12,192,384]{2,1,0:T(8,128)} %copy-done.2), kind=kOutput, calls=%fused_computation.312 | convolution fusion | flops 116198016 | bytes 5612544 | tf_op jit(solution)/shard_map/hrs,rhd->shd/dot_general | solution.py:58
  344.9 2.3 multiply_reduce_fusion
  348.4 3.2 fusion.70
  364.4 2.5 convolution_convert_fusion.2
  382.9 8.2 %collective-permute-done.36 = bf16[24,2048]{1,0:T(8,128)(2,1)S(1)} collective-permute-done((bf16[24,2048]{1,0:T(8,128)(2,1)S(1)}, bf16[24,2048]{1,0:T(8,128)(2,1)S(1)}, u32[]{:S(2)}, u32[]{:S(2)}) %collective-permute-start.36) | collective-permute-done | bytes 98336 | tf_op jit(solution)/shard_map/ppermute | solution.py:83
  392.9 5.8 %collective-permute-done.38 = bf16[24,2048]{1,0:T(8,128)(2,1)S(1)} collective-permute-done((bf16[24,2048]{1,0:T(8,128)(2,1)S(1)}, bf16[24,2048]{1,0:T(8,128)(2,1)S(1)}, u32[]{:S(2)}, u32[]{:S(2)}) %collective-permute-start.38) | collective-permute-done | bytes 98336 | tf_op jit(solution)/shard_map/ppermute | solution.py:83
  400.8 2.5 collective-permute-done.37
  404.3 4.2 fusion.102
  410.1 2.1 fusion.14
  435.2 2.0 fusion.65
  437.3 10.4 %collective-permute-done.19 = bf16[2,2,2,24,2304]{4,3,0,2,1:T(8,128)(2,1)S(1)} collective-permute-done((bf16[2,2,2,24,2304]{4,3,0,2,1:T(8,128)(2,1)S(1)}, bf16[2,2,2,24,2304]{4,3,0,2,1:T(8,128)(2,1)S(1)}, u32[]{:S(2)}, u32[]{:S(2)}) %collective-permute-start.19) | collective-permute-done | bytes 884768 | tf_op jit(solution)/shard_map/ppermute | solution.py:83
  459.5 3.4 collective-permute-start.24
  468.5 5.0 collective-permute-done.24
  475.7 2.7 collective-permute-done.23
  486.6 2.1 collective-permute-start.25
  492.7 6.1 %collective-permute-done.27 = bf16[2,24,2304]{2,1,0:T(8,128)(2,1)S(1)} collective-permute-done((bf16[2,24,2304]{2,1,0:T(8,128)(2,1)S(1)}, bf16[2,24,2304]{2,1,0:T(8,128)(2,1)S(1)}, u32[]{:S(2)}, u32[]{:S(2)}) %collective-permute-start.27) | collective-permute-done | bytes 221216 | tf_op jit(solution)/shard_map/ppermute | solution.py:83
  504.0 3.0 collective-permute-start.29
  (482 shorter events, 185.5 us)
Async XLA Ops:
  7.3 134.3 %all-gather.2.cloned.1.call-start = ((), (), s32[]{:S(2)}) async-start(), calls=%async_computation | async-start | bytes 19464192 | tf_op jit(solution)/shard_map/all_gather | solution.py:169
  14.2 131.1 %collective-permute-start.1 = (bf16[128,768]{1,0:T(8,128)(2,1)S(1)}, bf16[128,768]{1,0:T(8,128)(2,1)S(1)}, u32[]{:S(2)}, u32[]{:S(2)}) collective-permute-start(bf16[128,768]{1,0:T(8,128)(2,1)S(1)} %bitcast.379), channel_id=1, source_target_pairs={{0,1},{1,0},{2,3},{3,2},{4,5},{5,4},{6,7},{7,6},{8,9},{9,8},{10,11... | collective-permute-start | bytes 589832 | tf_op jit(solution)/shard_map/ppermute | solution.py:83
  17.3 12.8 %collective-permute-start = (bf16[192,768]{1,0:T(8,128)(2,1)S(1)}, bf16[192,768]{1,0:T(8,128)(2,1)S(1)}, u32[]{:S(2)}, u32[]{:S(2)}) collective-permute-start(bf16[192,768]{1,0:T(8,128)(2,1)S(1)} %bitcast.342), channel_id=1, source_target_pairs={{0,1},{1,0},{2,3},{3,2},{4,5},{5,4},{6,7},{7,6},{8,9},{9,8},{10,11... | collective-permute-start | bytes 884744 | tf_op jit(solution)/shard_map/ppermute | solution.py:83
  30.5 114.7 %copy-start.62 = (bf16[384,768]{1,0:T(8,128)(2,1)}, bf16[384,768]{1,0:T(8,128)(2,1)S(1)}, u32[]{:S(2)}) copy-start(bf16[384,768]{1,0:T(8,128)(2,1)S(1)} %fusion.60) | copy-start | bytes 1769476
  196.4 27.6 %collective-permute-start.2 = (bf16[2,2,2,2,24,2048]{5,4,2,3,0,1:T(8,128)(2,1)}, bf16[2,2,2,2,24,2048]{5,4,2,3,0,1:T(8,128)(2,1)}, u32[]{:S(2)}, u32[]{:S(2)}) collective-permute-start(bf16[2,2,2,2,24,2048]{5,4,2,3,0,1:T(8,128)(2,1)} %bitcast.329), channel_id=1, source_target_pairs={{0,2},{1,3},{2,0},{3,1},{4,6},{5,7},{6,4},{7,5},{8,10},{9,11},{10,... | collective-permute-start | bytes 4718600 | tf_op jit(solution)/shard_map/ppermute | solution.py:83
  200.7 24.5 %collective-permute-start.3 = (bf16[2,2,2,2,24,2048]{5,4,2,3,0,1:T(8,128)(2,1)}, bf16[2,2,2,2,24,2048]{5,4,2,3,0,1:T(8,128)(2,1)}, u32[]{:S(2)}, u32[]{:S(2)}) collective-permute-start(bf16[2,2,2,2,24,2048]{5,4,2,3,0,1:T(8,128)(2,1)} %bitcast.328), channel_id=1, source_target_pairs={{0,2},{1,3},{2,0},{3,1},{4,6},{5,7},{6,4},{7,5},{8,10},{9,11},{10,... | collective-permute-start | bytes 4718600 | tf_op jit(solution)/shard_map/ppermute | solution.py:83
  204.9 22.8 %collective-permute-start.4 = (bf16[2,2,2,2,24,2048]{5,4,2,3,0,1:T(8,128)(2,1)}, bf16[2,2,2,2,24,2048]{5,4,2,3,0,1:T(8,128)(2,1)}, u32[]{:S(2)}, u32[]{:S(2)}) collective-permute-start(bf16[2,2,2,2,24,2048]{5,4,2,3,0,1:T(8,128)(2,1)} %bitcast.327), channel_id=1, source_target_pairs={{0,2},{1,3},{2,0},{3,1},{4,6},{5,7},{6,4},{7,5},{8,10},{9,11},{10,... | collective-permute-start | bytes 4718600 | tf_op jit(solution)/shard_map/ppermute | solution.py:83
  220.0 28.0 %copy-start.25 = (f32[192,768]{1,0:T(8,128)}, f32[192,768]{1,0:T(8,128)S(1)}, u32[]{:S(2)}) copy-start(f32[192,768]{1,0:T(8,128)S(1)} %fusion.95) | copy-start | bytes 1769476
  233.9 41.5 %collective-permute-start.5 = (bf16[2,2,2,24,2048]{4,3,2,0,1:T(8,128)(2,1)}, bf16[2,2,2,24,2048]{4,3,2,0,1:T(8,128)(2,1)}, u32[]{:S(2)}, u32[]{:S(2)}) collective-permute-start(bf16[2,2,2,24,2048]{4,3,2,0,1:T(8,128)(2,1)} %fusion.90), channel_id=1, source_target_pairs={{0,1},{1,0},{2,3},{3,2},{4,5},{5,4},{6,7},{7,6},{8,9},{9,8},{10,11... | collective-permute-start | bytes 2359304 | tf_op jit(solution)/shard_map/ppermute | solution.py:83
  239.8 36.9 %collective-permute-start.6 = (bf16[2,2,2,24,2048]{4,3,1,2,0:T(8,128)(2,1)}, bf16[2,2,2,24,2048]{4,3,1,2,0:T(8,128)(2,1)}, u32[]{:S(2)}, u32[]{:S(2)}) collective-permute-start(bf16[2,2,2,24,2048]{4,3,1,2,0:T(8,128)(2,1)} %select_bitcast_fusion.3), channel_id=1, source_target_pairs={{0,4},{1,5},{2,6},{3,7},{4,0},{5,1},{6,2},{7,3},{8,12},{9,13},{10,... | collective-permute-start | bytes 2359304 | tf_op jit(solution)/shard_map/ppermute | solution.py:83
  244.4 34.7 %collective-permute-start.7 = (bf16[2,2,2,24,2048]{4,3,1,2,0:T(8,128)(2,1)}, bf16[2,2,2,24,2048]{4,3,1,2,0:T(8,128)(2,1)}, u32[]{:S(2)}, u32[]{:S(2)}) collective-permute-start(bf16[2,2,2,24,2048]{4,3,1,2,0:T(8,128)(2,1)} %select_bitcast_fusion.2), channel_id=1, source_target_pairs={{0,8},{1,9},{2,10},{3,11},{4,12},{5,13},{6,14},{7,15},{8,0},{9,1},... | collective-permute-start | bytes 2359304 | tf_op jit(solution)/shard_map/ppermute | solution.py:83
  261.4 10.6 %collective-permute-start.12 = (bf16[128,1536]{0,1:T(8,128)(2,1)S(1)}, bf16[128,1536]{0,1:T(8,128)(2,1)S(1)}, u32[]{:S(2)}, u32[]{:S(2)}) collective-permute-start(bf16[128,1536]{0,1:T(8,128)(2,1)S(1)} %slice.431), channel_id=1, source_target_pairs={{0,1},{1,0},{2,3},{3,2},{4,5},{5,4},{6,7},{7,6},{8,9},{9,8},{10,11... | collective-permute-start | bytes 1179656 | tf_op jit(solution)/shard_map/ppermute | solution.py:83
  266.9 14.1 %copy-start.8 = (bf16[2,2,2,2,24,2048]{5,4,2,3,0,1:T(8,128)(2,1)S(1)}, bf16[2,2,2,2,24,2048]{5,4,2,3,0,1:T(8,128)(2,1)}, u32[]{:S(2)}) copy-start(bf16[2,2,2,2,24,2048]{5,4,2,3,0,1:T(8,128)(2,1)} %copy-done.7) | copy-start | bytes 4718596
  266.9 143.2 %collective-permute-start.15 = (bf16[2,2,2,2,24,2304]{5,4,0,2,1,3:T(8,128)(2,1)}, bf16[2,2,2,2,24,2304]{5,4,0,2,1,3:T(8,128)(2,1)}, u32[]{:S(2)}, u32[]{:S(2)}) collective-permute-start(bf16[2,2,2,2,24,2304]{5,4,0,2,1,3:T(8,128)(2,1)} %bitcast.325), channel_id=1, source_target_pairs={{0,2},{1,3},{2,0},{3,1},{4,6},{5,7},{6,4},{7,5},{8,10},{9,11},{10,... | collective-permute-start | bytes 5308424 | tf_op jit(solution)/shard_map/ppermute | solution.py:83
  285.4 27.4 %collective-permute-start.8 = (bf16[2,2,24,2048]{3,2,0,1:T(8,128)(2,1)}, bf16[2,2,24,2048]{3,2,0,1:T(8,128)(2,1)}, u32[]{:S(2)}, u32[]{:S(2)}) collective-permute-start(bf16[2,2,24,2048]{3,2,0,1:T(8,128)(2,1)} %fusion.111), channel_id=1, source_target_pairs={{0,4},{1,5},{2,6},{3,7},{4,0},{5,1},{6,2},{7,3},{8,12},{9,13},{10,... | collective-permute-start | bytes 1179656 | tf_op jit(solution)/shard_map/ppermute | solution.py:83
  290.4 23.6 %collective-permute-start.9 = (bf16[2,2,24,2048]{3,2,0,1:T(8,128)(2,1)}, bf16[2,2,24,2048]{3,2,0,1:T(8,128)(2,1)}, u32[]{:S(2)}, u32[]{:S(2)}) collective-permute-start(bf16[2,2,24,2048]{3,2,0,1:T(8,128)(2,1)} %select_bitcast_fusion.7), channel_id=1, source_target_pairs={{0,8},{1,9},{2,10},{3,11},{4,12},{5,13},{6,14},{7,15},{8,0},{9,1},... | collective-permute-start | bytes 1179656 | tf_op jit(solution)/shard_map/ppermute | solution.py:83
  295.6 20.9 %collective-permute-start.10 = (bf16[2,2,24,2048]{3,2,0,1:T(8,128)(2,1)}, bf16[2,2,24,2048]{3,2,0,1:T(8,128)(2,1)}, u32[]{:S(2)}, u32[]{:S(2)}) collective-permute-start(bf16[2,2,24,2048]{3,2,0,1:T(8,128)(2,1)} %select_bitcast_fusion.6), channel_id=1, source_target_pairs={{0,16},{1,17},{2,18},{3,19},{4,20},{5,21},{6,22},{7,23},{8,24},{9,... | collective-permute-start | bytes 1179656 | tf_op jit(solution)/shard_map/ppermute | solution.py:83
  312.8 13.4 %copy-start.44 = (bf16[2,2,2,24,2048]{4,3,1,2,0:T(8,128)(2,1)S(1)}, bf16[2,2,2,24,2048]{4,3,1,2,0:T(8,128)(2,1)}, u32[]{:S(2)}) copy-start(bf16[2,2,2,24,2048]{4,3,1,2,0:T(8,128)(2,1)} %copy-done.43) | copy-start | bytes 2359300
  312.8 101.1 %collective-permute-start.16 = (bf16[2,2,2,2,24,1536]{5,4,0,2,1,3:T(8,128)(2,1)}, bf16[2,2,2,2,24,1536]{5,4,0,2,1,3:T(8,128)(2,1)}, u32[]{:S(2)}, u32[]{:S(2)}) collective-permute-start(bf16[2,2,2,2,24,1536]{5,4,0,2,1,3:T(8,128)(2,1)} %copy_bitcast_fusion.10), channel_id=1, source_target_pairs={{0,2},{1,3},{2,0},{3,1},{4,6},{5,7},{6,4},{7,5},{8,10},{9,11},{10,... | collective-permute-start | bytes 3538952 | tf_op jit(solution)/shard_map/ppermute | solution.py:83
  321.4 50.6 %collective-permute-start.34 = (bf16[2,24,2048]{2,1,0:T(8,128)(2,1)}, bf16[2,24,2048]{2,1,0:T(8,128)(2,1)}, u32[]{:S(2)}, u32[]{:S(2)}) collective-permute-start(bf16[2,24,2048]{2,1,0:T(8,128)(2,1)} %select_bitcast_fusion.12), channel_id=1, source_target_pairs={{0,8},{1,9},{2,10},{3,11},{4,12},{5,13},{6,14},{7,15},{8,0},{9,1},... | collective-permute-start | bytes 589832 | tf_op jit(solution)/shard_map/ppermute | solution.py:83
  325.0 48.3 %collective-permute-start.33 = (bf16[2,24,2048]{2,1,0:T(8,128)(2,1)}, bf16[2,24,2048]{2,1,0:T(8,128)(2,1)}, u32[]{:S(2)}, u32[]{:S(2)}) collective-permute-start(bf16[2,24,2048]{2,1,0:T(8,128)(2,1)} %select_bitcast_fusion.11), channel_id=1, source_target_pairs={{0,16},{1,17},{2,18},{3,19},{4,20},{5,21},{6,22},{7,23},{8,24},{9,... | collective-permute-start | bytes 589832 | tf_op jit(solution)/shard_map/ppermute | solution.py:83
  329.3 48.0 %collective-permute-start.35 = (bf16[2,24,2048]{2,1,0:T(8,128)(2,1)}, bf16[2,24,2048]{2,1,0:T(8,128)(2,1)}, u32[]{:S(2)}, u32[]{:S(2)}) collective-permute-start(bf16[2,24,2048]{2,1,0:T(8,128)(2,1)} %select_bitcast_fusion.10), channel_id=1, source_target_pairs={{0,1},{1,0},{2,3},{3,2},{4,5},{5,4},{6,7},{7,6},{8,9},{9,8},{10,11... | collective-permute-start | bytes 589832 | tf_op jit(solution)/shard_map/ppermute | solution.py:83
  372.0 44.7 %collective-permute-start.14 = (bf16[2,2,2,2,24,2304]{5,4,0,2,1,3:T(8,128)(2,1)}, bf16[2,2,2,2,24,2304]{5,4,0,2,1,3:T(8,128)(2,1)S(1)}, u32[]{:S(2)}, u32[]{:S(2)}) collective-permute-start(bf16[2,2,2,2,24,2304]{5,4,0,2,1,3:T(8,128)(2,1)} %bitcast.326), channel_id=1, source_target_pairs={{0,2},{1,3},{2,0},{3,1},{4,6},{5,7},{6,4},{7,5},{8,10},{9,11},{10,... | collective-permute-start | bytes 5308424 | tf_op jit(solution)/shard_map/ppermute | solution.py:83
  373.3 30.8 %collective-permute-start.11 = (bf16[192,1536]{1,0:T(8,128)(2,1)S(1)}, bf16[192,1536]{1,0:T(8,128)(2,1)S(1)}, u32[]{:S(2)}, u32[]{:S(2)}) collective-permute-start(bf16[192,1536]{1,0:T(8,128)(2,1)S(1)} %pad_maximum_fusion.5), channel_id=1, source_target_pairs={{0,1},{1,0},{2,3},{3,2},{4,5},{5,4},{6,7},{7,6},{8,9},{9,8},{10,11... | collective-permute-start | bytes 1769480 | tf_op jit(solution)/shard_map/ppermute | solution.py:83
  380.2 23.9 %copy-start.50 = (f32[192,768]{1,0:T(8,128)S(1)}, f32[192,768]{1,0:T(8,128)}, u32[]{:S(2)}) copy-start(f32[192,768]{1,0:T(8,128)} %copy.175) | copy-start | bytes 1769476
  380.2 23.9 %copy-start.51 = (f32[192,768]{1,0:T(8,128)S(1)}, f32[192,768]{1,0:T(8,128)}, u32[]{:S(2)}) copy-start(f32[192,768]{1,0:T(8,128)} %copy.174) | copy-start | bytes 1769476
  381.3 9.8 %collective-permute-start.36 = (bf16[24,2048]{1,0:T(8,128)(2,1)S(1)}, bf16[24,2048]{1,0:T(8,128)(2,1)S(1)}, u32[]{:S(2)}, u32[]{:S(2)}) collective-permute-start(bf16[24,2048]{1,0:T(8,128)(2,1)S(1)} %select_bitcast_fusion.17), channel_id=1, source_target_pairs={{0,1},{1,0},{2,3},{3,2},{4,5},{5,4},{6,7},{7,6},{8,9},{9,8},{10,11... | collective-permute-start | bytes 294920 | tf_op jit(solution)/shard_map/ppermute | solution.py:83
  391.1 7.5 %collective-permute-start.38 = (bf16[24,2048]{1,0:T(8,128)(2,1)S(1)}, bf16[24,2048]{1,0:T(8,128)(2,1)S(1)}, u32[]{:S(2)}, u32[]{:S(2)}) collective-permute-start(bf16[24,2048]{1,0:T(8,128)(2,1)S(1)} %select_bitcast_fusion.15), channel_id=1, source_target_pairs={{0,16},{1,17},{2,18},{3,19},{4,20},{5,21},{6,22},{7,23},{8,24},{9,... | collective-permute-start | bytes 294920 | tf_op jit(solution)/shard_map/ppermute | solution.py:83
  398.7 4.6 collective-permute-start.37
  408.5 4.9 collective-permute-start.13
  422.1 11.9 %collective-permute-start.20 = (bf16[2,2,2,24,1536]{4,3,0,2,1:T(8,128)(2,1)}, bf16[2,2,2,24,1536]{4,3,0,2,1:T(8,128)(2,1)}, u32[]{:S(2)}, u32[]{:S(2)}) collective-permute-start(bf16[2,2,2,24,1536]{4,3,0,2,1:T(8,128)(2,1)} %fusion.103), channel_id=1, source_target_pairs={{0,8},{1,9},{2,10},{3,11},{4,12},{5,13},{6,14},{7,15},{8,0},{9,1},... | collective-permute-start | bytes 1769480 | tf_op jit(solution)/shard_map/ppermute | solution.py:83
  425.8 23.3 %collective-permute-start.18 = (bf16[2,2,2,24,2304]{4,3,0,2,1:T(8,128)(2,1)}, bf16[2,2,2,24,2304]{4,3,0,2,1:T(8,128)(2,1)}, u32[]{:S(2)}, u32[]{:S(2)}) collective-permute-start(bf16[2,2,2,24,2304]{4,3,0,2,1:T(8,128)(2,1)} %select_bitcast_fusion.1), channel_id=1, source_target_pairs={{0,1},{1,0},{2,3},{3,2},{4,5},{5,4},{6,7},{7,6},{8,9},{9,8},{10,11... | collective-permute-start | bytes 2654216 | tf_op jit(solution)/shard_map/ppermute | solution.py:83
  429.7 18.0 %collective-permute-start.19 = (bf16[2,2,2,24,2304]{4,3,0,2,1:T(8,128)(2,1)S(1)}, bf16[2,2,2,24,2304]{4,3,0,2,1:T(8,128)(2,1)S(1)}, u32[]{:S(2)}, u32[]{:S(2)}) collective-permute-start(bf16[2,2,2,24,2304]{4,3,0,2,1:T(8,128)(2,1)S(1)} %copy.189), channel_id=1, source_target_pairs={{0,4},{1,5},{2,6},{3,7},{4,0},{5,1},{6,2},{7,3},{8,12},{9,13},{10,... | collective-permute-start | bytes 2654216 | tf_op jit(solution)/shard_map/ppermute | solution.py:83
  431.9 1.2 collective-permute-start.17
  433.1 16.0 %copy-start.85 = (f32[2688]{0:T(1024)}, f32[2688]{0:T(1024)S(1)}, u32[]{:S(2)}) copy-start(f32[2688]{0:T(1024)S(1)} %add.530) | copy-start | bytes 32260
  457.3 21.6 %collective-permute-start.22 = (bf16[2,2,24,2304]{3,2,0,1:T(8,128)(2,1)}, bf16[2,2,24,2304]{3,2,0,1:T(8,128)(2,1)}, u32[]{:S(2)}, u32[]{:S(2)}) collective-permute-start(bf16[2,2,24,2304]{3,2,0,1:T(8,128)(2,1)} %select_bitcast_fusion.5), channel_id=1, source_target_pairs={{0,4},{1,5},{2,6},{3,7},{4,0},{5,1},{6,2},{7,3},{8,12},{9,13},{10,... | collective-permute-start | bytes 1327112 | tf_op jit(solution)/shard_map/ppermute | solution.py:83
  459.5 13.9 %collective-permute-start.24 = (bf16[2,2,24,1536]{3,2,0,1:T(8,128)(2,1)}, bf16[2,2,24,1536]{3,2,0,1:T(8,128)(2,1)}, u32[]{:S(2)}, u32[]{:S(2)}) collective-permute-start(bf16[2,2,24,1536]{3,2,0,1:T(8,128)(2,1)} %fusion.116), channel_id=1, source_target_pairs={{0,16},{1,17},{2,18},{3,19},{4,20},{5,21},{6,22},{7,23},{8,24},{9,... | collective-permute-start | bytes 884744 | tf_op jit(solution)/shard_map/ppermute | solution.py:83
  464.3 3.7 collective-permute-start.21
  465.0 17.7 %copy-start.35 = (bf16[2,2,2,24,2304]{4,3,0,2,1:T(8,128)(2,1)S(1)}, bf16[2,2,2,24,2304]{4,3,0,2,1:T(8,128)(2,1)}, u32[]{:S(2)}) copy-start(bf16[2,2,2,24,2304]{4,3,0,2,1:T(8,128)(2,1)} %copy-done.34) | copy-start | bytes 2654212
  465.1 13.3 %collective-permute-start.23 = (bf16[2,2,24,2304]{3,2,0,1:T(8,128)(2,1)S(1)}, bf16[2,2,24,2304]{3,2,0,1:T(8,128)(2,1)S(1)}, u32[]{:S(2)}, u32[]{:S(2)}) collective-permute-start(bf16[2,2,24,2304]{3,2,0,1:T(8,128)(2,1)S(1)} %select_bitcast_fusion.4), channel_id=1, source_target_pairs={{0,8},{1,9},{2,10},{3,11},{4,12},{5,13},{6,14},{7,15},{8,0},{9,1},... | collective-permute-start | bytes 1327112 | tf_op jit(solution)/shard_map/ppermute | solution.py:83
  484.4 14.9 %collective-permute-start.26 = (bf16[2,24,2304]{2,1,0:T(8,128)(2,1)S(1)}, bf16[2,24,2304]{2,1,0:T(8,128)(2,1)S(1)}, u32[]{:S(2)}, u32[]{:S(2)}) collective-permute-start(bf16[2,24,2304]{2,1,0:T(8,128)(2,1)S(1)} %select_bitcast_fusion.9), channel_id=1, source_target_pairs={{0,8},{1,9},{2,10},{3,11},{4,12},{5,13},{6,14},{7,15},{8,0},{9,1},... | collective-permute-start | bytes 663560 | tf_op jit(solution)/shard_map/ppermute | solution.py:83
  484.4 7.8 %collective-permute-start.28 = (bf16[2,24,1536]{2,1,0:T(8,128)(2,1)S(1)}, bf16[2,24,1536]{2,1,0:T(8,128)(2,1)S(1)}, u32[]{:S(2)}, u32[]{:S(2)}) collective-permute-start(bf16[2,24,1536]{2,1,0:T(8,128)(2,1)S(1)} %fusion.122), channel_id=1, source_target_pairs={{0,1},{1,0},{2,3},{3,2},{4,5},{5,4},{6,7},{7,6},{8,9},{9,8},{10,11... | collective-permute-start | bytes 442376 | tf_op jit(solution)/shard_map/ppermute | solution.py:83
  486.6 5.0 collective-permute-start.25
  488.9 9.9 %collective-permute-start.27 = (bf16[2,24,2304]{2,1,0:T(8,128)(2,1)S(1)}, bf16[2,24,2304]{2,1,0:T(8,128)(2,1)S(1)}, u32[]{:S(2)}, u32[]{:S(2)}) collective-permute-start(bf16[2,24,2304]{2,1,0:T(8,128)(2,1)S(1)} %select_bitcast_fusion.8), channel_id=1, source_target_pairs={{0,16},{1,17},{2,18},{3,19},{4,20},{5,21},{6,22},{7,23},{8,24},{9,... | collective-permute-start | bytes 663560 | tf_op jit(solution)/shard_map/ppermute | solution.py:83
  503.1 10.2 %collective-permute-start.30 = (bf16[24,2304]{1,0:T(8,128)(2,1)S(1)}, bf16[24,2304]{1,0:T(8,128)(2,1)S(1)}, u32[]{:S(2)}, u32[]{:S(2)}) collective-permute-start(bf16[24,2304]{1,0:T(8,128)(2,1)S(1)} %select_bitcast_fusion.14), channel_id=1, source_target_pairs={{0,16},{1,17},{2,18},{3,19},{4,20},{5,21},{6,22},{7,23},{8,24},{9,... | collective-permute-start | bytes 331784 | tf_op jit(solution)/shard_map/ppermute | solution.py:83
  503.1 8.2 %collective-permute-start.31 = (bf16[24,1536]{1,0:T(8,128)(2,1)S(1)}, bf16[24,1536]{1,0:T(8,128)(2,1)S(1)}, u32[]{:S(2)}, u32[]{:S(2)}) collective-permute-start(bf16[24,1536]{1,0:T(8,128)(2,1)S(1)} %select_bitcast_fusion.18), channel_id=1, source_target_pairs={{0,4},{1,5},{2,6},{3,7},{4,0},{5,1},{6,2},{7,3},{8,12},{9,13},{10,... | collective-permute-start | bytes 221192 | tf_op jit(solution)/shard_map/ppermute | solution.py:83
  504.0 5.8 %collective-permute-start.29 = (f32[2688]{0:T(1024)S(1)}, f32[2688]{0:T(1024)S(1)}, u32[]{:S(2)}, u32[]{:S(2)}) collective-permute-start(f32[2688]{0:T(1024)S(1)} %broadcast_select_fusion), channel_id=1, source_target_pairs={{0,16},{1,17},{2,18},{3,19},{4,20},{5,21},{6,22},{7,23},{8,24},{9,... | collective-permute-start | bytes 32264 | tf_op jit(solution)/shard_map/ppermute | solution.py:83
  507.1 4.9 collective-permute-start.32
  (102 other events, 494.7 us)
Sparse Core Ops, SparseCore 0:
  14.3 127.2 all-gather.1

commit v3 on v1

--- a/solution.py
+++ b/solution.py
@@ -102,6 +102,10 @@
         left.remove(bit)
         values = total.astype(jnp.bfloat16) if left else total
     return values
+
+
+def after(never, values, other):
+    return jnp.where(never, other[0, 0].astype(values.dtype), values)
 
 
 def full_sum(values, bits, devices):
@@ -134,6 +138,8 @@
     my_seq = lax.axis_index("seq")
     index = lax.axis_index("dp") * 2 + my_seq
 
+    never = segment_ids[0, 0] < 0
+
     def scattered(values, turn):
         return scatter_sum(values, bit_order(bits, turn), devices, index)
 
@@ -213,7 +219,6 @@
     )
     grad_out = cotangent[0].astype(jnp.float32)
     grad_branch = cotangent[0]
-    ff_out_grad = scattered(outer_rows(grad_branch, mixed_act), 0)
     grad_mixed = jnp.einsum(
         "td,df->tf", grad_branch, ff_out_all, preferred_element_type=jnp.float32
     )
@@ -221,9 +226,13 @@
     grad_gate, grad_up = gate_pull(grad_mixed)
     grad_gate = grad_gate.astype(jnp.bfloat16)
     grad_up = grad_up.astype(jnp.bfloat16)
-    gate_grad = scattered(outer_rows(normed_three, grad_gate), 1)
-    up_grad = scattered(outer_rows(normed_three, grad_up), 2)
     grad_pre = jnp.concatenate([grad_gate, grad_up], 1)
+    ff_grads = jnp.concatenate(
+        [outer_rows(normed_three, grad_pre), outer_rows(grad_branch, mixed_act)], 1
+    )
+    grad_pre = after(never, grad_pre, ff_grads)
+    ff_grads = lax.psum_scatter(ff_grads, axes, scatter_dimension=0, tiled=True)
+    ff_grads = ff_grads.astype(jnp.float32)
     grad_normed = jnp.einsum("tk,ck->tc", grad_pre, ff_in_all, preferred_element_type=jnp.float32)
     norm_value, norm_pull = jax.vjp(rms_scaled, hidden_two, norm_gains[2])
     grad_resid, gain_three = norm_pull(grad_normed)
@@ -283,11 +292,16 @@
     keys_low = grad_keys.astype(jnp.bfloat16)
     values_low = grad_values.astype(jnp.bfloat16)
     grad_queries_one = grad_queries.reshape(tok_count, model_width).astype(jnp.bfloat16)
-    in_grads = [
-        scattered(outer_rows(normed_both, values_low), 0),
-        scattered(outer_rows(normed_both, keys_low), 1),
-        scattered(outer_rows(normed_both[:tok_count], grad_queries_one), 2),
-    ]
+    in_grads = scattered(
+        jnp.concatenate(
+            [
+                outer_rows(normed_both[:tok_count], grad_queries_one),
+                outer_rows(normed_both, jnp.concatenate([keys_low, values_low], 1)),
+            ],
+            1,
+        ),
+        0,
+    )
     other_part = swap_bit(
         jnp.concatenate([keys_low[tok_count:], values_low[tok_count:]], 1), 0, devices
     ).astype(jnp.float32)
@@ -310,13 +324,13 @@
         encoder_grad[None],
         small[: 3 * model_width].reshape(3, model_width),
         small[3 * model_width :].reshape(rel_table.shape),
-        jnp.concatenate([in_grads[2], in_grads[1], in_grads[0]], 1),
+        in_grads,
         middle_grads[:, model_width:],
         middle_grads[:, :model_width],
         cross_grads[:, : 2 * model_width],
         cross_grads[:, 2 * model_width :],
-        jnp.concatenate([gate_grad, up_grad], 1),
-        ff_out_grad,
+        ff_grads[:, : 2 * FF],
+        ff_grads[:, 2 * FF :],
     )
 
 

time: 522 us -> 469 us (0.90)
  starting transfers between devices: 53.3 us -> 19.1 us
  local copies, waits for them, and re-layouts: 71.7 us -> 57.2 us
  waiting for transfers between devices: 232 us -> 225 us
    ppermute x49 -> x24, starting transfers between devices: 53.2 us -> 19 us  [swap_bit(): lax.ppermute(values, axes, [(at, at ^ 1 << bit) for at in range(devices)])]
    ppermute x49 -> x24, waiting for transfers between devices: 116 us -> 83.3 us  [swap_bit(): lax.ppermute(values, axes, [(at, at ^ 1 << bit) for at in range(devices)])]
    reduce_scatter x0 -> x1, waiting for transfers between devices: none -> 30.2 us  [local(): ff_grads = lax.psum_scatter(ff_grads, axes, scatter_dimension=0, tiled=True)]
    dynamic_slice x7 -> x2, local copies, waits for them, and re-layouts: 10.8 us -> 3.01 us  [scatter_sum(): kept = lax.dynamic_index_in_dim(values, mine, place, keepdims=False)]
    convert_element_type x32 -> x12, other arithmetic: 14.8 us -> 7.98 us  [scatter_sum(): values = total.astype(jnp.bfloat16) if left else total]
    dynamic_slice x7 -> x2, local copies, waits for them, and re-layouts: 9.26 us -> 2.63 us  [scatter_sum(): sent = lax.dynamic_index_in_dim(values, 1 - mine, place, keepdims=False)]
    unnamed x189 -> x169, local copies, waits for them, and re-layouts: 15.6 us -> 12 us
    dot_general x10 -> x8, matrix products: 13.4 us -> 14.7 us  [outer_rows(): jnp.einsum('tc,tk->ck', left, right, preferred_element_type=jnp.float32)]
  transfers between devices with their start and end apart: 50 -> 26, of which waited for: 28 -> 12; matrix products, arithmetic and copies ran while one was open for 18% -> 18% of each run, Pallas kernels for 0% -> 0%
where the time goes in v3:
time: 469 us; the launch traced here: 463 us
  waiting for transfers between devices  225 us (48%)
  matrix products  113 us (24%)
  local copies, waits for them, and re-layouts  57.2 us (12%)
  other arithmetic  31.1 us (7%)
  starting transfers between devices  19.1 us (4%)
  between operations  16.3 us (3%)
    all_gather x1, waiting for transfers between devices, local(): lax.all_gather(jnp.concatenate(shards, 1), axes, axis=0, tiled=True)  112 us
    ppermute x24, waiting for transfers between devices, swap_bit(): lax.ppermute(values, axes, [(at, at ^ 1 << bit) for at in range(devices)])  83.3 us
    reduce_scatter x1, waiting for transfers between devices, local(): ff_grads = lax.psum_scatter(ff_grads, axes, scatter_dimension=0, tiled=True)  30.2 us
    ppermute x24, starting transfers between devices, swap_bit(): lax.ppermute(values, axes, [(at, at ^ 1 << bit) for at in range(devices)])  19 us
    dot_general x8, matrix products, outer_rows(): jnp.einsum('tc,tk->ck', left, right, preferred_element_type=jnp.float32)  14.7 us
    unnamed x169, local copies, waits for them, and re-layouts  12 us
    dot_general x2, matrix products, attend_forward(): jnp.einsum('hrs,shd->rhd', weights_full.astype(jnp.bfloat16), values, pre...  11.4 us
    dot_general x2, matrix products, attend_backward(): jnp.einsum('hrs,rhd->shd', weights_low, grad_context, preferred_element_t...  10.8 us
  transfers between devices with their start and end apart: 26, of which 12 were waited for; matrix products, arithmetic and copies ran while one was open for 18% of the time, Pallas kernels for 0%

profile of v3, /device:TPU:0, one launch (start us, length us, event | category | flops | bytes accessed | tf_op | source)
XLA Modules:
  0.0 462.5 jit_solution(8983134814921997761)
XLA Ops:
  14.1 3.0 collective-permute-start
  24.2 5.1 %fusion.3 = f32[192,384,12]{1,2,0:T(8,128)} fusion(s32[192,384]{1,0:T(8,128)S(1)} %subtract_maximum_fusion, s32[32]{0:T(128)S(1)} %get-tuple-element.58, s32[32]{0:T(128)S(1)} %get-tuple-element.57, f32[32,12]{0,1:T(8,128)S(1)} %copy-done), kind=kOutput, calls=%fused_computation.5 | convolution fusion | flops 346816512 | bytes 3835648 | tf_op jit(solution)/shard_map/bij,bh->hij/dot_general | solution.py:36
  29.7 111.9 %all-gather.2.cloned.1.call-done = bf16[768,12288]{1,0:T(8,128)(2,1)} async-done(((bf16[24,12288]{1,0:T(8,128)(2,1)}), bf16[768,12288]{1,0:T(8,128)(2,1)}) %all-gather.2.cloned.1.call-update) | async-done | bytes 18874384 | tf_op jit(solution)/shard_map/all_gather | solution.py:147
  141.6 3.6 convolution_convert_fusion.1
  147.4 4.1 fusion.16
  151.6 3.2 fusion.132
  154.7 2.5 copy.98
  157.3 2.7 convolution_convert_fusion.5
  162.8 8.2 %convolution_convert_fusion.13 = bf16[12,64,192]{2,1,0:T(8,128)(2,1)} fusion(bf16[384,12,64]{0,2,1:T(8,128)(2,1)} %bitcast.234, f32[12,192]{1,0:T(8,128)} %get-tuple-element.74, f32[12,192,384]{2,1,0:T(8,128)} %copy-done.4), kind=kOutput, calls=%fused_computation.94 | convolution fusion | flops 116050560 | bytes 4432896 | tf_op jit(solution)/shard_map/hrs,shd->rhd/dot_general | solution.py:47
  171.0 2.0 multiply_reduce_fusion.7
  173.8 2.5 convolution_convert_fusion.16
  180.1 3.8 fusion.133
  183.9 3.2 convolution_convert_fusion.12
  187.0 2.1 multiply_reduce_fusion.6
  189.1 4.4 fusion.6
  193.6 5.0 %fusion.39 = (bf16[192,2048]{1,0:T(8,128)(2,1)S(1)}, bf16[192,2048]{1,0:T(8,128)(2,1)S(1)}, bf16[192,2048]{1,0:T(8,128)(2,1)}) fusion(f32[192,4096]{1,0:T(8,128)S(1)} %fusion.6, bf16[768,12288]{1,0:T(8,128)(2,1)} %all-gather.2.cloned.1.call-done, bf16[1,192,768]{2,1,0:T(8,128)(2,1)S(1)} %copy-done.51), kind=kOutput, calls=%fused_computation.72 | convolution fusion | flops 615776256 | bytes 8945664 | tf_op jit(solution)/shard_map/td,df->tf/dot_general | solution.py:222
  198.6 2.1 convolution_convert_fusion
  201.2 7.3 %multiply_reduce_fusion.2 = (f32[768]{0:T(1024)}, f32[192]{0:T(256)S(1)}, f32[192,768]{1,0:T(8,128)S(1)}) fusion(f32[192,768]{1,0:T(8,128)S(1)} %get-tuple-element.81, f32[192]{0:T(256)S(1)} %fusion.112, f32[768]{0:T(1024)S(1)} %get-tuple-element.54, bf16[768,12288]{1,0:T(8,128)(2,1)} %all-gather.2.cloned.1.call-done, pred[]{:T(512)} %bitcast.18, ...), kind=kOutput, calls=%fused_computation.157 | convolution fusion | flops 1212775424 | bytes 9052672 | tf_op jit(solution)/shard_map/tk,ck->tc/dot_general | solution.py:236
  209.6 2.5 convolution_convert_fusion.15
  214.1 3.2 multiply_reduce_fusion.1
  218.8 2.2 multiply_reduce_fusion.3
  222.0 2.5 convolution_convert_fusion.14
  226.5 8.7 %fusion.134 = (bf16[384,12,64]{0,2,1:T(8,128)(2,1)}, f32[384,12,64]{0,2,1:T(8,128)}) fusion(bf16[192,12,64]{0,2,1:T(8,128)(2,1)} %bitcast.240, f32[12,192]{1,0:T(8,128)} %get-tuple-element.74, f32[12,192,384]{2,1,0:T(8,128)} %copy-done.4), kind=kOutput, calls=%fused_computation.245 | convolution fusion | flops 116198016 | bytes 5612544 | tf_op jit(solution)/shard_map/hrs,rhd->shd/dot_general | solution.py:58
  235.2 2.3 multiply_reduce_fusion
  237.5 2.7 multiply_convert_fusion
  244.2 2.1 fusion.94
  246.3 4.2 fusion.64
  252.9 2.6 convolution_convert_fusion.9
  269.2 2.4 copy.114
  271.6 2.6 convolution_convert_fusion.4
  279.8 3.1 copy.117
  292.4 4.7 %fusion.92 = (f32[768]{0:T(1024)S(1)}, f32[192]{0:T(256)}, f32[192,768]{1,0:T(8,128)}) fusion(f32[192]{0:T(256)S(1)} %copy-done.70, bf16[1,192,768]{2,1,0:T(8,128)(2,1)S(1)} %copy-done.29, f32[768]{0:T(1024)S(1)} %get-tuple-element.55, bf16[768,12288]{1,0:T(8,128)(2,1)} %all-gather.2.cloned.1.call-done, bf16[192,1536]{1,0:T(8,128)(2,1)S(1)} %fusion.56, ...), kind=kOutput, calls=%fused_computation.151 | convolution fusion | flops 682277952 | bytes 5316096 | tf_op jit(solution)/shard_map/tk,ck->tc/dot_general | solution.py:315
  299.2 4.0 pad_maximum_fusion
  304.3 4.0 fusion.61
  311.1 4.1 fusion.50
  316.7 10.0 %collective-permute-done.7 = f32[2688]{0:T(1024)S(1)} collective-permute-done((f32[2688]{0:T(1024)S(1)}, f32[2688]{0:T(1024)S(1)}, u32[]{:S(2)}, u32[]{:S(2)}) %collective-permute-start.7) | collective-permute-done | bytes 10784 | tf_op jit(solution)/shard_map/ppermute | solution.py:83
  329.1 2.1 collective-permute-done.8
  335.6 2.0 fusion.14
  339.1 9.4 %collective-permute-done.16 = bf16[2,2,24,1536]{3,2,1,0:T(8,128)(2,1)S(1)} collective-permute-done((bf16[2,2,24,1536]{3,2,1,0:T(8,128)(2,1)S(1)}, bf16[2,2,24,1536]{3,2,1,0:T(8,128)(2,1)S(1)}, u32[]{:S(2)}, u32[]{:S(2)}) %collective-permute-start.16) | collective-permute-done | bytes 294944 | tf_op jit(solution)/shard_map/ppermute | solution.py:83
  349.7 1.9 fusion.15
  351.6 2.9 collective-permute-done.17
  356.5 7.9 %collective-permute-done.18 = bf16[24,1536]{1,0:T(8,128)(2,1)S(1)} collective-permute-done((bf16[24,1536]{1,0:T(8,128)(2,1)S(1)}, bf16[24,1536]{1,0:T(8,128)(2,1)S(1)}, u32[]{:S(2)}, u32[]{:S(2)}) %collective-permute-start.18) | collective-permute-done | bytes 73760 | tf_op jit(solution)/shard_map/ppermute | solution.py:83
  365.6 17.3 %collective-permute-done.10 = bf16[2,2,2,24,2304]{4,3,0,1,2:T(8,128)(2,1)S(1)} collective-permute-done((bf16[2,2,2,24,2304]{4,3,0,1,2:T(8,128)(2,1)S(1)}, bf16[2,2,2,24,2304]{4,3,0,1,2:T(8,128)(2,1)S(1)}, u32[]{:S(2)}, u32[]{:S(2)}) %collective-permute-start.10) | collective-permute-done | bytes 884768 | tf_op jit(solution)/shard_map/ppermute | solution.py:83
  384.7 6.5 %collective-permute-done.21 = bf16[2,2,24,2304]{3,2,1,0:T(8,128)(2,1)S(1)} collective-permute-done((bf16[2,2,24,2304]{3,2,1,0:T(8,128)(2,1)S(1)}, bf16[2,2,24,2304]{3,2,1,0:T(8,128)(2,1)S(1)}, u32[]{:S(2)}, u32[]{:S(2)}) %collective-permute-start.21) | collective-permute-done | bytes 442400 | tf_op jit(solution)/shard_map/ppermute | solution.py:83
  391.4 11.9 %collective-permute-done.11 = bf16[2,2,24,2304]{3,2,0,1:T(8,128)(2,1)S(1)} collective-permute-done((bf16[2,2,24,2304]{3,2,0,1:T(8,128)(2,1)S(1)}, bf16[2,2,24,2304]{3,2,0,1:T(8,128)(2,1)S(1)}, u32[]{:S(2)}, u32[]{:S(2)}) %collective-permute-start.11) | collective-permute-done | bytes 442400 | tf_op jit(solution)/shard_map/ppermute | solution.py:83
  404.0 6.6 %collective-permute-done.12 = bf16[2,24,2304]{2,1,0:T(8,128)(2,1)S(1)} collective-permute-done((bf16[2,24,2304]{2,1,0:T(8,128)(2,1)S(1)}, bf16[2,24,2304]{2,1,0:T(8,128)(2,1)S(1)}, u32[]{:S(2)}, u32[]{:S(2)}) %collective-permute-start.12) | collective-permute-done | bytes 221216 | tf_op jit(solution)/shard_map/ppermute | solution.py:83
  412.4 8.7 %collective-permute-done.13 = bf16[24,2304]{1,0:T(8,128)(2,1)S(1)} collective-permute-done((bf16[24,2304]{1,0:T(8,128)(2,1)S(1)}, bf16[24,2304]{1,0:T(8,128)(2,1)S(1)}, u32[]{:S(2)}, u32[]{:S(2)}) %collective-permute-start.13) | collective-permute-done | bytes 110624 | tf_op jit(solution)/shard_map/ppermute | solution.py:83
  421.8 30.2 %reduce-scatter.2.cloned.1.call-done = bf16[24,6144]{1,0:T(8,128)(2,1)} async-done(((bf16[768,6144]{1,0:T(8,128)(2,1)}), bf16[24,6144]{1,0:T(8,128)(2,1)}) %reduce-scatter.2.cloned.1.call-update) | async-done | bytes 294928 | tf_op jit(solution)/shard_map/reduce_scatter | solution.py:234
  (316 shorter events, 94.4 us)
Async XLA Ops:
  7.2 17.0 %copy-start = (f32[32,12]{0,1:T(8,128)S(1)}, f32[32,12]{0,1:T(8,128)}, u32[]{:S(2)}) copy-start(f32[32,12]{0,1:T(8,128)} %param.19) | copy-start | bytes 4612
  7.2 134.4 %all-gather.2.cloned.1.call-start = ((), (), s32[]{:S(2)}) async-start(), calls=%async_computation.1 | async-start | bytes 19464192 | tf_op jit(solution)/shard_map/all_gather | solution.py:147
  14.0 437.9 %reduce-scatter.2.cloned.1.call-start = ((), (), s32[]{:S(2)}) async-start(), calls=%async_computation.2 | async-start | bytes 9732096 | tf_op jit(solution)/shard_map/reduce_scatter | solution.py:234
  14.1 15.2 %collective-permute-start = (bf16[192,768]{1,0:T(8,128)(2,1)}, bf16[192,768]{1,0:T(8,128)(2,1)S(1)}, u32[]{:S(2)}, u32[]{:S(2)}) collective-permute-start(bf16[192,768]{1,0:T(8,128)(2,1)} %bitcast.208), channel_id=1, source_target_pairs={{0,1},{1,0},{2,3},{3,2},{4,5},{5,4},{6,7},{7,6},{8,9},{9,8},{10,11... | collective-permute-start | bytes 884744 | tf_op jit(solution)/shard_map/ppermute | solution.py:83
  17.1 140.2 %collective-permute-start.1 = (bf16[128,768]{1,0:T(8,128)(2,1)}, bf16[128,768]{1,0:T(8,128)(2,1)}, u32[]{:S(2)}, u32[]{:S(2)}) collective-permute-start(bf16[128,768]{1,0:T(8,128)(2,1)} %bitcast.245), channel_id=1, source_target_pairs={{0,1},{1,0},{2,3},{3,2},{4,5},{5,4},{6,7},{7,6},{8,9},{9,8},{10,11... | collective-permute-start | bytes 589832 | tf_op jit(solution)/shard_map/ppermute | solution.py:83
  20.8 8.5 %copy-start.75 = (s32[32]{0:T(128)}, s32[32]{0:T(128)S(1)}, u32[]{:S(2)}) copy-start(s32[32]{0:T(128)S(1)} %get-tuple-element.57) | copy-start | bytes 388
  20.8 8.5 %copy-start.77 = (s32[32]{0:T(128)}, s32[32]{0:T(128)S(1)}, u32[]{:S(2)}) copy-start(s32[32]{0:T(128)S(1)} %get-tuple-element.58) | copy-start | bytes 388
  29.7 115.5 %copy-start.48 = (bf16[384,768]{1,0:T(8,128)(2,1)}, bf16[384,768]{1,0:T(8,128)(2,1)S(1)}, u32[]{:S(2)}) copy-start(bf16[384,768]{1,0:T(8,128)(2,1)S(1)} %fusion.55) | copy-start | bytes 1769476
  154.7 80.4 %copy-start.3 = (f32[12,192,384]{2,1,0:T(8,128)}, f32[12,192,384]{2,1,0:T(8,128)S(1)}, u32[]{:S(2)}) copy-start(f32[12,192,384]{2,1,0:T(8,128)S(1)} %get-tuple-element.75) | copy-start | bytes 10616836
  173.6 10.3 %copy-start.66 = (f32[192]{0:T(256)}, f32[192]{0:T(256)S(1)}, u32[]{:S(2)}) copy-start(f32[192]{0:T(256)S(1)} %fusion.111) | copy-start | bytes 2308
  189.1 19.5 %copy-start.17 = (f32[192,768]{1,0:T(8,128)}, f32[192,768]{1,0:T(8,128)S(1)}, u32[]{:S(2)}) copy-start(f32[192,768]{1,0:T(8,128)S(1)} %get-tuple-element.81) | copy-start | bytes 1769476
  200.7 7.9 %copy-start.2 = (bf16[768,4096]{1,0:T(8,128)(2,1)}, bf16[768,4096]{1,0:T(8,128)(2,1)S(1)}, u32[]{:S(2)}) copy-start(bf16[768,4096]{1,0:T(8,128)(2,1)S(1)} %convolution_convert_fusion) | copy-start | bytes 18874372
  260.1 6.8 %copy-start.13 = (f32[12,64,256]{2,1,0:T(8,128)S(1)}, f32[12,64,256]{2,1,0:T(8,128)}, u32[]{:S(2)}) copy-start(f32[12,64,256]{2,1,0:T(8,128)} %fusion.136) | copy-start | bytes 2359300
  260.1 6.8 %copy-start.40 = (f32[12,64,256]{2,1,0:T(8,128)S(1)}, f32[12,64,256]{2,1,0:T(8,128)}, u32[]{:S(2)}) copy-start(f32[12,64,256]{2,1,0:T(8,128)} %fusion.94) | copy-start | bytes 2359300
  265.5 25.2 %collective-permute-start.2 = (bf16[192,1536]{1,0:T(8,128)(2,1)}, bf16[192,1536]{1,0:T(8,128)(2,1)}, u32[]{:S(2)}, u32[]{:S(2)}) collective-permute-start(bf16[192,1536]{1,0:T(8,128)(2,1)} %pad_maximum_fusion.9), channel_id=1, source_target_pairs={{0,1},{1,0},{2,3},{3,2},{4,5},{5,4},{6,7},{7,6},{8,9},{9,8},{10,11... | collective-permute-start | bytes 1769480 | tf_op jit(solution)/shard_map/ppermute | solution.py:83
  267.0 7.2 %copy-start.24 = (bf16[256,1536]{0,1:T(8,128)(2,1)}, bf16[256,1536]{0,1:T(8,128)(2,1)S(1)}, u32[]{:S(2)}) copy-start(bf16[256,1536]{0,1:T(8,128)(2,1)S(1)} %fusion.35) | copy-start | bytes 2359300
  267.8 43.2 %collective-permute-start.3 = (bf16[128,1536]{0,1:T(8,128)(2,1)}, bf16[128,1536]{0,1:T(8,128)(2,1)}, u32[]{:S(2)}, u32[]{:S(2)}) collective-permute-start(bf16[128,1536]{0,1:T(8,128)(2,1)} %slice.187), channel_id=1, source_target_pairs={{0,1},{1,0},{2,3},{3,2},{4,5},{5,4},{6,7},{7,6},{8,9},{9,8},{10,11... | collective-permute-start | bytes 1179656 | tf_op jit(solution)/shard_map/ppermute | solution.py:83
  277.3 72.4 %collective-permute-start.9 = (bf16[2,2,2,2,24,2304]{5,4,0,1,2,3:T(8,128)(2,1)}, bf16[2,2,2,2,24,2304]{5,4,0,1,2,3:T(8,128)(2,1)}, u32[]{:S(2)}, u32[]{:S(2)}) collective-permute-start(bf16[2,2,2,2,24,2304]{5,4,0,1,2,3:T(8,128)(2,1)} %bitcast.196), channel_id=1, source_target_pairs={{0,2},{1,3},{2,0},{3,1},{4,6},{5,7},{6,4},{7,5},{8,10},{9,11},{10,... | collective-permute-start | bytes 5308424 | tf_op jit(solution)/shard_map/ppermute | solution.py:83
  284.1 25.0 %collective-permute-start.14 = (bf16[2,2,2,2,24,1536]{5,4,3,2,1,0:T(8,128)(2,1)}, bf16[2,2,2,2,24,1536]{5,4,3,2,1,0:T(8,128)(2,1)}, u32[]{:S(2)}, u32[]{:S(2)}) collective-permute-start(bf16[2,2,2,2,24,1536]{5,4,3,2,1,0:T(8,128)(2,1)} %dynamic-slice_bitcast_fusion), channel_id=1, source_target_pairs={{0,2},{1,3},{2,0},{3,1},{4,6},{5,7},{6,4},{7,5},{8,10},{9,11},{10,... | collective-permute-start | bytes 3538952 | tf_op jit(solution)/shard_map/ppermute | solution.py:83
  289.2 46.4 %collective-permute-start.19 = (bf16[2,2,2,2,24,2304]{5,4,3,0,1,2:T(8,128)(2,1)}, bf16[2,2,2,2,24,2304]{5,4,3,0,1,2:T(8,128)(2,1)}, u32[]{:S(2)}, u32[]{:S(2)}) collective-permute-start(bf16[2,2,2,2,24,2304]{5,4,3,0,1,2:T(8,128)(2,1)} %bitcast.195), channel_id=1, source_target_pairs={{0,2},{1,3},{2,0},{3,1},{4,6},{5,7},{6,4},{7,5},{8,10},{9,11},{10,... | collective-permute-start | bytes 5308424 | tf_op jit(solution)/shard_map/ppermute | solution.py:83
  289.6 9.6 %slice-start = ((s8[6291456]{0:T(1024)(128)(4,1)}), s8[4194304]{0:T(1024)(128)(4,1)S(1)}, s32[]{:S(2)}) async-start(s8[6291456]{0:T(1024)(128)(4,1)} %bitcast.198), calls=%async_computation.3 | async-start | bytes 8388608
  290.7 8.5 %slice-start.1 = ((s8[6291456]{0:T(1024)(128)(4,1)}), s8[2097152]{0:T(1024)(128)(4,1)S(1)}, s32[]{:S(2)}) async-start(s8[6291456]{0:T(1024)(128)(4,1)} %bitcast.198), calls=%async_computation.4 | async-start | bytes 4194304
  297.1 6.1 %copy-start.65 = (f32[768]{0:T(1024)}, f32[768]{0:T(1024)S(1)}, u32[]{:S(2)}) copy-start(f32[768]{0:T(1024)S(1)} %get-tuple-element.52) | copy-start | bytes 9220
  297.7 5.6 %collective-permute-start.4 = (f32[2688]{0:T(1024)}, f32[2688]{0:T(1024)}, u32[]{:S(2)}, u32[]{:S(2)}) collective-permute-start(f32[2688]{0:T(1024)} %pad_maximum_fusion.13), channel_id=1, source_target_pairs={{0,1},{1,0},{2,3},{3,2},{4,5},{5,4},{6,7},{7,6},{8,9},{9,8},{10,11... | collective-permute-start | bytes 32264 | tf_op jit(solution)/shard_map/ppermute | solution.py:83
  304.0 4.3 collective-permute-start.5
  308.4 6.8 %collective-permute-start.6 = (f32[2688]{0:T(1024)S(1)}, f32[2688]{0:T(1024)S(1)}, u32[]{:S(2)}, u32[]{:S(2)}) collective-permute-start(f32[2688]{0:T(1024)S(1)} %add.257), channel_id=1, source_target_pairs={{0,4},{1,5},{2,6},{3,7},{4,0},{5,1},{6,2},{7,3},{8,12},{9,13},{10,... | collective-permute-start | bytes 32264 | tf_op jit(solution)/shard_map/ppermute | solution.py:83
  310.8 5.9 %copy-start.69 = (f32[192]{0:T(256)S(1)}, f32[192]{0:T(256)}, u32[]{:S(2)}) copy-start(f32[192]{0:T(256)} %copy-done.68) | copy-start | bytes 2308
  310.8 5.8 %copy-start.74 = (f32[192]{0:T(256)S(1)}, f32[192]{0:T(256)}, u32[]{:S(2)}) copy-start(f32[192]{0:T(256)} %get-tuple-element.53) | copy-start | bytes 2308
  310.8 17.2 %copy-start.30 = (bf16[1,192,768]{2,1,0:T(8,128)(2,1)S(1)}, bf16[1,192,768]{2,1,0:T(8,128)(2,1)}, u32[]{:S(2)}) copy-start(bf16[1,192,768]{2,1,0:T(8,128)(2,1)} %param.14) | copy-start | bytes 884740
  310.8 17.2 %copy-start.54 = (f32[192,768]{1,0:T(8,128)S(1)}, f32[192,768]{1,0:T(8,128)}, u32[]{:S(2)}) copy-start(f32[192,768]{1,0:T(8,128)} %get-tuple-element.92) | copy-start | bytes 1769476
  310.9 17.2 %copy-start.71 = (f32[192]{0:T(256)S(1)}, f32[192]{0:T(256)}, u32[]{:S(2)}) copy-start(f32[192]{0:T(256)} %fusion.113) | copy-start | bytes 2308
  310.9 21.8 %collective-permute-start.15 = (bf16[2,2,2,24,1536]{4,3,2,1,0:T(8,128)(2,1)S(1)}, bf16[2,2,2,24,1536]{4,3,2,1,0:T(8,128)(2,1)}, u32[]{:S(2)}, u32[]{:S(2)}) collective-permute-start(bf16[2,2,2,24,1536]{4,3,2,1,0:T(8,128)(2,1)S(1)} %dynamic-slice_bitcast_fusion.3), channel_id=1, source_target_pairs={{0,8},{1,9},{2,10},{3,11},{4,12},{5,13},{6,14},{7,15},{8,0},{9,1},... | collective-permute-start | bytes 1769480 | tf_op jit(solution)/shard_map/ppermute | solution.py:83
  315.2 20.5 %copy-start.16 = (bf16[2,2,2,1,2,24,2304]{6,5,4,3,2,1,0:T(8,128)(2,1)S(1)}, bf16[2,2,2,1,2,24,2304]{6,5,4,3,2,1,0:T(8,128)(2,1)}, u32[]{:S(2)}) copy-start(bf16[2,2,2,1,2,24,2304]{6,5,4,3,2,1,0:T(8,128)(2,1)} %get-tuple-element.61) | copy-start | bytes 5308420
  315.2 11.5 %collective-permute-start.7 = (f32[2688]{0:T(1024)S(1)}, f32[2688]{0:T(1024)S(1)}, u32[]{:S(2)}, u32[]{:S(2)}) collective-permute-start(f32[2688]{0:T(1024)S(1)} %add.258), channel_id=1, source_target_pairs={{0,8},{1,9},{2,10},{3,11},{4,12},{5,13},{6,14},{7,15},{8,0},{9,1},... | collective-permute-start | bytes 32264 | tf_op jit(solution)/shard_map/ppermute | solution.py:83
  326.6 4.6 collective-permute-start.8
  334.1 14.4 %collective-permute-start.16 = (bf16[2,2,24,1536]{3,2,1,0:T(8,128)(2,1)S(1)}, bf16[2,2,24,1536]{3,2,1,0:T(8,128)(2,1)S(1)}, u32[]{:S(2)}, u32[]{:S(2)}) collective-permute-start(bf16[2,2,24,1536]{3,2,1,0:T(8,128)(2,1)S(1)} %dynamic-slice_bitcast_fusion.6), channel_id=1, source_target_pairs={{0,16},{1,17},{2,18},{3,19},{4,20},{5,21},{6,22},{7,23},{8,24},{9,... | collective-permute-start | bytes 884744 | tf_op jit(solution)/shard_map/ppermute | solution.py:83
  337.6 12.0 %copy-start.15 = (bf16[2,2,2,1,2,24,2304]{6,5,4,3,2,1,0:T(8,128)(2,1)S(1)}, bf16[2,2,2,1,2,24,2304]{6,5,4,3,2,1,0:T(8,128)(2,1)}, u32[]{:S(2)}) copy-start(bf16[2,2,2,1,2,24,2304]{6,5,4,3,2,1,0:T(8,128)(2,1)} %get-tuple-element.63) | copy-start | bytes 5308420
  337.7 27.4 %collective-permute-start.20 = (bf16[2,2,2,24,2304]{4,3,2,0,1:T(8,128)(2,1)S(1)}, bf16[2,2,2,24,2304]{4,3,2,0,1:T(8,128)(2,1)S(1)}, u32[]{:S(2)}, u32[]{:S(2)}) collective-permute-start(bf16[2,2,2,24,2304]{4,3,2,0,1:T(8,128)(2,1)S(1)} %dynamic-slice_bitcast_fusion.1), channel_id=1, source_target_pairs={{0,4},{1,5},{2,6},{3,7},{4,0},{5,1},{6,2},{7,3},{8,12},{9,13},{10,... | collective-permute-start | bytes 2654216 | tf_op jit(solution)/shard_map/ppermute | solution.py:83
  348.7 5.8 %collective-permute-start.17 = (bf16[2,24,1536]{2,1,0:T(8,128)(2,1)S(1)}, bf16[2,24,1536]{2,1,0:T(8,128)(2,1)S(1)}, u32[]{:S(2)}, u32[]{:S(2)}) collective-permute-start(bf16[2,24,1536]{2,1,0:T(8,128)(2,1)S(1)} %dynamic-slice_bitcast_fusion.9), channel_id=1, source_target_pairs={{0,1},{1,0},{2,3},{3,2},{4,5},{5,4},{6,7},{7,6},{8,9},{9,8},{10,11... | collective-permute-start | bytes 442376 | tf_op jit(solution)/shard_map/ppermute | solution.py:83
  354.6 9.9 %collective-permute-start.18 = (bf16[24,1536]{1,0:T(8,128)(2,1)S(1)}, bf16[24,1536]{1,0:T(8,128)(2,1)S(1)}, u32[]{:S(2)}, u32[]{:S(2)}) collective-permute-start(bf16[24,1536]{1,0:T(8,128)(2,1)S(1)} %dynamic-slice_bitcast_fusion.12), channel_id=1, source_target_pairs={{0,4},{1,5},{2,6},{3,7},{4,0},{5,1},{6,2},{7,3},{8,12},{9,13},{10,... | collective-permute-start | bytes 221192 | tf_op jit(solution)/shard_map/ppermute | solution.py:83
  355.8 27.1 %collective-permute-start.10 = (bf16[2,2,2,24,2304]{4,3,0,1,2:T(8,128)(2,1)S(1)}, bf16[2,2,2,24,2304]{4,3,0,1,2:T(8,128)(2,1)S(1)}, u32[]{:S(2)}, u32[]{:S(2)}) collective-permute-start(bf16[2,2,2,24,2304]{4,3,0,1,2:T(8,128)(2,1)S(1)} %dynamic-slice_bitcast_fusion.2), channel_id=1, source_target_pairs={{0,1},{1,0},{2,3},{3,2},{4,5},{5,4},{6,7},{7,6},{8,9},{9,8},{10,11... | collective-permute-start | bytes 2654216 | tf_op jit(solution)/shard_map/ppermute | solution.py:83
  365.4 25.8 %collective-permute-start.21 = (bf16[2,2,24,2304]{3,2,1,0:T(8,128)(2,1)S(1)}, bf16[2,2,24,2304]{3,2,1,0:T(8,128)(2,1)S(1)}, u32[]{:S(2)}, u32[]{:S(2)}) collective-permute-start(bf16[2,2,24,2304]{3,2,1,0:T(8,128)(2,1)S(1)} %dynamic-slice_bitcast_fusion.4), channel_id=1, source_target_pairs={{0,8},{1,9},{2,10},{3,11},{4,12},{5,13},{6,14},{7,15},{8,0},{9,1},... | collective-permute-start | bytes 1327112 | tf_op jit(solution)/shard_map/ppermute | solution.py:83
  383.2 20.1 %collective-permute-start.11 = (bf16[2,2,24,2304]{3,2,0,1:T(8,128)(2,1)S(1)}, bf16[2,2,24,2304]{3,2,0,1:T(8,128)(2,1)S(1)}, u32[]{:S(2)}, u32[]{:S(2)}) collective-permute-start(bf16[2,2,24,2304]{3,2,0,1:T(8,128)(2,1)S(1)} %dynamic-slice_bitcast_fusion.5), channel_id=1, source_target_pairs={{0,4},{1,5},{2,6},{3,7},{4,0},{5,1},{6,2},{7,3},{8,12},{9,13},{10,... | collective-permute-start | bytes 1327112 | tf_op jit(solution)/shard_map/ppermute | solution.py:83
  391.3 12.2 %collective-permute-start.22 = (bf16[2,24,2304]{2,1,0:T(8,128)(2,1)S(1)}, bf16[2,24,2304]{2,1,0:T(8,128)(2,1)S(1)}, u32[]{:S(2)}, u32[]{:S(2)}) collective-permute-start(bf16[2,24,2304]{2,1,0:T(8,128)(2,1)S(1)} %dynamic-slice_bitcast_fusion.7), channel_id=1, source_target_pairs={{0,16},{1,17},{2,18},{3,19},{4,20},{5,21},{6,22},{7,23},{8,24},{9,... | collective-permute-start | bytes 663560 | tf_op jit(solution)/shard_map/ppermute | solution.py:83
  403.2 52.0 %copy-start.1 = (f32[32,12]{0,1:T(8,128)S(1)}, f32[32,12]{0,1:T(8,128)}, u32[]{:S(2)}) copy-start(f32[32,12]{0,1:T(8,128)} %param.19) | copy-start | bytes 4612
  403.4 7.2 %collective-permute-start.12 = (bf16[2,24,2304]{2,1,0:T(8,128)(2,1)S(1)}, bf16[2,24,2304]{2,1,0:T(8,128)(2,1)S(1)}, u32[]{:S(2)}, u32[]{:S(2)}) collective-permute-start(bf16[2,24,2304]{2,1,0:T(8,128)(2,1)S(1)} %dynamic-slice_bitcast_fusion.8), channel_id=1, source_target_pairs={{0,8},{1,9},{2,10},{3,11},{4,12},{5,13},{6,14},{7,15},{8,0},{9,1},... | collective-permute-start | bytes 663560 | tf_op jit(solution)/shard_map/ppermute | solution.py:83
  403.6 7.5 %collective-permute-start.23 = (bf16[24,2304]{1,0:T(8,128)(2,1)S(1)}, bf16[24,2304]{1,0:T(8,128)(2,1)S(1)}, u32[]{:S(2)}, u32[]{:S(2)}) collective-permute-start(bf16[24,2304]{1,0:T(8,128)(2,1)S(1)} %dynamic-slice_bitcast_fusion.10), channel_id=1, source_target_pairs={{0,1},{1,0},{2,3},{3,2},{4,5},{5,4},{6,7},{7,6},{8,9},{9,8},{10,11... | collective-permute-start | bytes 331784 | tf_op jit(solution)/shard_map/ppermute | solution.py:83
  410.6 10.4 %collective-permute-start.13 = (bf16[24,2304]{1,0:T(8,128)(2,1)S(1)}, bf16[24,2304]{1,0:T(8,128)(2,1)S(1)}, u32[]{:S(2)}, u32[]{:S(2)}) collective-permute-start(bf16[24,2304]{1,0:T(8,128)(2,1)S(1)} %dynamic-slice_bitcast_fusion.11), channel_id=1, source_target_pairs={{0,16},{1,17},{2,18},{3,19},{4,20},{5,21},{6,22},{7,23},{8,24},{9,... | collective-permute-start | bytes 331784 | tf_op jit(solution)/shard_map/ppermute | solution.py:83
  (59 other events, 150.2 us)
Sparse Core Ops, SparseCore 0:
  14.2 127.4 all-gather.1
  303.4 148.5 reduce-scatter.1
